TPU v7x, 256 devices: a whole 4x4x8 slice. The times are simulated.
256 devices in a mesh: head: 4 (over x_hi, core), inner: 16 (over x_lo, z), outer: 4 (over y).
Axes of the slice: x: 4 (x_hi: 2, x_lo: 2; x = x_hi * 2 + x_lo), y: 4, z: 8, core: 2. Of those that a mesh axis runs over, the one named last changes fastest.
Arguments:
- queries: bfloat16 [14336, 4096], P(('head', 'inner', 'outer')), may hold values from -400 to 400
- keys: bfloat16 [14336, 1024], P(('head', 'inner', 'outer')), may hold values from -14 to 14
- values: bfloat16 [14336, 1024], P(('head', 'inner', 'outer')), may hold values from -6 to 6
- span_order: int32 [256], replicated, may hold values from 0 to 255, each once
- block_pattern: int32 [256, 256], replicated, may hold values 0 or 1
- summary_flag: int32 [256], replicated, may hold values 0 or 1
Outputs:
- attended: bfloat16 [14336, 4096], P(('head', 'inner', 'outer'))
All inputs are finite; a program needn't handle non-finite values.
Results may differ from a plain program's by a relative error of at most 0.0064.
Values may be sent and summed in bfloat16 or wider, within the bound.
No kernel may reach another device: no remote copies, remote signals or barrier semaphores. Data moves between devices by JAX's collectives and lax.ppermute only.
A program may use at most 64 MiB of HBM per device.

v0:
```python
import math

import jax
import jax.numpy as jnp
from jax import lax
from jax.experimental import pallas as pl
from jax.experimental.pallas import tpu as pltpu
from jax.sharding import Mesh
from jax.sharding import PartitionSpec as P

HEAD = 128
GROUP = 4
SPAN = 56
PADDED = 64
ROWS = GROUP * SPAN
EXTRA = 16
BATCH = 4
TOGETHER = 4
NEG = -1e30
LOG2E = math.log2(math.e)
SCORE_SCALE = LOG2E / math.sqrt(HEAD)
SUMMARY_BIAS = math.log2(SPAN)

HEADS = ("xhi", "xlo", "ylo")
ALL = ("xhi", "core", "xlo", "z", "yhi", "ylo")


def nt_dot(a, b):
    return lax.dot_general(a, b, (((1,), (1,)), ((), ())), preferred_element_type=jnp.float32)


def attend_kernel(
    list_ref, count_ref, own_ref, turn_ref, q_ref, bias_ref, *refs, pieces, together
):
    piece_refs, (out_ref, kv_ref, sums, base, held, turned) = refs[:pieces], refs[pieces:]
    key_spans = kv_ref.shape[0]
    query_spans = q_ref.shape[0]

    first = 0
    for piece_ref in piece_refs:

        def prepare(j, carry, piece_ref=piece_ref, first=first):
            block = piece_ref[j]
            kv_ref[first + j] = block
            sums[pl.ds(first + j, 1), :] = jnp.sum(block.astype(jnp.float32), axis=0, keepdims=True)
            return carry

        lax.fori_loop(0, piece_ref.shape[0], prepare, 0, unroll=8)
        first += piece_ref.shape[0]
    summary = (sums[...] / math.sqrt(SPAN)).astype(jnp.bfloat16)

    gap = jnp.zeros((PADDED - SPAN, HEAD), jnp.bfloat16)
    blank = jnp.zeros((PADDED - SPAN, ROWS), jnp.float32)
    key = lax.broadcasted_iota(jnp.int32, (SPAN, ROWS), 0)
    query = lax.broadcasted_iota(jnp.int32, (SPAN, ROWS), 1) % SPAN
    causal = jnp.where(key <= query, 0.0, NEG)
    eye = (
        lax.broadcasted_iota(jnp.int32, (ROWS, ROWS), 0) == lax.broadcasted_iota(jnp.int32, (ROWS, ROWS), 1)
    ).astype(jnp.bfloat16)

    def pile(slots, lanes):
        blocks = []
        for slot in slots:
            blocks += [kv_ref[slot, :, lanes], gap]
        return jnp.concatenate(blocks, axis=0)

    def high(x):
        return jnp.max(x.reshape(x.shape[0] // 8, 8, x.shape[1]), axis=0)

    def add(x):
        return jnp.sum(x.reshape(x.shape[0] // 8, 8, x.shape[1]), axis=0)

    def mixed_by(values, weight):
        return lax.dot_general(
            values, weight.astype(jnp.bfloat16), (((0,), (0,)), ((), ())), preferred_element_type=jnp.float32
        )

    key_lanes, value_lanes = pl.ds(0, HEAD), pl.ds(HEAD, HEAD)

    def some_spans(i, carry):
        spans = [turn_ref[i * together + u] for u in range(together)]
        counts = [count_ref[s] for s in spans]
        owns = [own_ref[s] for s in spans]
        most = counts[0]
        for c in counts[1:]:
            most = jnp.maximum(most, c)
        batches = (most + BATCH - 1) // BATCH

        for u, s in enumerate(spans):
            turned[u] = q_ref[s].T

        peaks = []
        for u, s in enumerate(spans):
            keys = jnp.concatenate([summary[:, :HEAD], pile([jnp.maximum(owns[u], 0)], key_lanes)], axis=0)
            scores = jnp.dot(keys, turned[u], preferred_element_type=jnp.float32) * SCORE_SCALE
            here = (lax.broadcasted_iota(jnp.int32, (bias_ref.shape[1], ROWS), 0) == s).astype(jnp.bfloat16)
            far = scores[:key_spans] + SUMMARY_BIAS + jnp.dot(bias_ref[...], here, preferred_element_type=jnp.float32)
            near = scores[key_spans : key_spans + SPAN] + (causal + jnp.where(owns[u] >= 0, 0.0, NEG))
            base[u, :key_spans] = far
            base[u, key_spans:] = near
            peaks.append(jnp.maximum(high(far), high(near)))

        def score(t, peaks):
            new = []
            for u, s in enumerate(spans):
                keys = pile([list_ref[s, t * BATCH + k] for k in range(BATCH)], key_lanes)
                scores = jnp.dot(keys, turned[u], preferred_element_type=jnp.float32) * SCORE_SCALE
                peak = peaks[u]
                for k in range(BATCH):
                    part = scores[k * PADDED : k * PADDED + SPAN]
                    part = part + jnp.where(t * BATCH + k < counts[u], 0.0, NEG)
                    held[u, t, k * SPAN : (k + 1) * SPAN] = part
                    peak = jnp.maximum(peak, high(part))
                new.append(peak)
            return tuple(new)

        peaks = lax.fori_loop(0, batches, score, tuple(peaks))
        peaks = [jnp.max(peak, axis=0, keepdims=True) for peak in peaks]

        state = []
        for u, s in enumerate(spans):
            weight = jnp.exp2(base[u] - peaks[u])
            values = jnp.concatenate([summary[:, HEAD:], pile([jnp.maximum(owns[u], 0)], value_lanes)], axis=0)
            total = add(weight)
            state.append((total, mixed_by(values, jnp.concatenate([weight, blank], axis=0))))

        def mix(t, state):
            new = []
            for u, s in enumerate(spans):
                total, mixed = state[u]
                values = pile([list_ref[s, t * BATCH + k] for k in range(BATCH)], value_lanes)
                weight = jnp.exp2(held[u, t] - peaks[u])
                total = total + add(weight)
                parts = []
                for k in range(BATCH):
                    parts += [weight[k * SPAN : (k + 1) * SPAN], blank]
                new.append((total, mixed + mixed_by(values, jnp.concatenate(parts, axis=0))))
            return tuple(new)

        state = lax.fori_loop(0, batches, mix, tuple(state))
        for u, s in enumerate(spans):
            total, mixed = state[u]
            total = jnp.sum(total, axis=0, keepdims=True)
            out_ref[s, :ROWS, :] = nt_dot(eye, (mixed / total).astype(jnp.bfloat16)).astype(jnp.bfloat16)
            level = peaks[u] + jnp.log2(total)
            first = level.astype(jnp.bfloat16).astype(jnp.float32)
            second = (level - first).astype(jnp.bfloat16).astype(jnp.float32)
            rows = jnp.concatenate([first, second, level - first - second, blank[:5]], axis=0)
            rows = jnp.concatenate([rows, jnp.zeros((8, 2 * HEAD - ROWS), jnp.float32)], axis=1)
            rows = jnp.concatenate([rows[:, :HEAD], rows[:, HEAD:]], axis=0)
            out_ref[s, ROWS:, :] = rows.astype(jnp.bfloat16)
        return carry

    lax.fori_loop(0, query_spans // together, some_spans, 0)


def attend(lists, counts, owns, turns, q, pieces, bias):
    query_spans, key_spans = q.shape[0], sum(piece.shape[0] for piece in pieces)
    vmem = pl.BlockSpec(memory_space=pltpu.VMEM)
    smem = pl.BlockSpec(memory_space=pltpu.SMEM)

    def kernel(*refs):
        attend_kernel(*refs, pieces=len(pieces), together=TOGETHER)

    return pl.pallas_call(
        kernel,
        out_shape=jax.ShapeDtypeStruct((query_spans, ROWS + EXTRA, HEAD), jnp.bfloat16),
        in_specs=[smem] * 4 + [vmem] * (2 + len(pieces)),
        out_specs=vmem,
        scratch_shapes=[
            pltpu.VMEM((key_spans, SPAN, 2 * HEAD), jnp.bfloat16),
            pltpu.VMEM((key_spans, 2 * HEAD), jnp.float32),
            pltpu.VMEM((TOGETHER, key_spans + SPAN, ROWS), jnp.float32),
            pltpu.VMEM((TOGETHER, key_spans // BATCH, BATCH * SPAN, ROWS), jnp.float32),
            pltpu.VMEM((TOGETHER, HEAD, ROWS), jnp.bfloat16),
        ],
        compiler_params=pltpu.CompilerParams(vmem_limit_bytes=48 * 1024 * 1024),
    )(lists, counts, owns, turns, q, bias, *pieces)


def combine_kernel(parts_ref, out_ref, *, pieces):
    heads = parts_ref.shape[0] // pieces
    three = (lax.broadcasted_iota(jnp.int32, (8, HEAD), 0) < 3).astype(jnp.bfloat16)

    def spread(rows):
        return lax.dot_general(rows, three, (((0,), (0,)), ((), ())), preferred_element_type=jnp.float32)

    for h in range(heads):
        levels = []
        for y in range(pieces):
            tail = parts_ref[h * pieces + y, ROWS:, :].astype(jnp.float32)
            both = [spread(tail[k * 8 : k * 8 + 8].astype(jnp.bfloat16)) for k in range(2)]
            levels.append(jnp.concatenate(both, axis=0)[:ROWS])
        peak = levels[0]
        for level in levels[1:]:
            peak = jnp.maximum(peak, level)
        total = jnp.zeros_like(peak)
        mixed = jnp.zeros_like(peak)
        for y in range(pieces):
            weight = jnp.exp2(levels[y] - peak)
            total = total + weight
            mixed = mixed + weight * parts_ref[h * pieces + y, :ROWS, :].astype(jnp.float32)
        mixed = (mixed / total)
        for g in range(GROUP):
            at = (h * GROUP + g) * HEAD
            out_ref[:, at : at + HEAD] = mixed[g * SPAN : (g + 1) * SPAN].astype(jnp.bfloat16)


def combine(parts, pieces):
    heads = parts.shape[0] // pieces
    vmem = pl.BlockSpec(memory_space=pltpu.VMEM)

    def kernel(parts_ref, out_ref):
        combine_kernel(parts_ref, out_ref, pieces=pieces)

    return pl.pallas_call(
        kernel,
        out_shape=jax.ShapeDtypeStruct((SPAN, heads * GROUP * HEAD), jnp.bfloat16),
        in_specs=[vmem],
        out_specs=vmem,
        compiler_params=pltpu.CompilerParams(vmem_limit_bytes=32 * 1024 * 1024),
    )(parts)


def tables(query_true, key_true, block_pattern, summary_flag):
    spans = block_pattern.shape[0]
    ids = jnp.arange(spans, dtype=jnp.int32)
    query_pick = (query_true[:, None] == ids[None, :]).astype(jnp.bfloat16)
    key_pick = (key_true[:, None] == ids[None, :]).astype(jnp.bfloat16)
    rows = jnp.dot(query_pick, block_pattern.astype(jnp.bfloat16), preferred_element_type=jnp.float32)
    pattern = nt_dot(rows.astype(jnp.bfloat16), key_pick) > 0.5
    flag = nt_dot((summary_flag == 1).astype(jnp.bfloat16)[None, :], key_pick) > 0.5
    earlier = key_true[None, :] < query_true[:, None]
    full = earlier & pattern
    bias = jnp.where(earlier & ~pattern & flag, 0.0, NEG).T.astype(jnp.bfloat16)
    slot = jnp.arange(key_true.shape[0], dtype=jnp.int32)
    upto = (slot[:, None] <= slot[None, :]).astype(jnp.bfloat16)
    rank = jnp.dot(full.astype(jnp.bfloat16), upto, preferred_element_type=jnp.float32).astype(jnp.int32) - 1
    hit = full[:, None, :] & (rank[:, None, :] == slot[None, :, None])
    lists = jnp.sum(jnp.where(hit, slot[None, None, :], 0), axis=2, dtype=jnp.int32)
    counts = jnp.sum(full.astype(jnp.int32), axis=1, dtype=jnp.int32)
    same = key_true[None, :] == query_true[:, None]
    owns = jnp.sum(jnp.where(same, slot[None, :] + 1, 0), axis=1, dtype=jnp.int32) - 1
    ids = jnp.arange(counts.shape[0], dtype=jnp.int32)
    ahead = (counts[None, :] > counts[:, None]) | ((counts[None, :] == counts[:, None]) & (ids[None, :] < ids[:, None]))
    place = jnp.sum(ahead.astype(jnp.int32), axis=1, dtype=jnp.int32)
    turns = jnp.sum(jnp.where(place[None, :] == ids[:, None], ids[None, :], 0), axis=1, dtype=jnp.int32)
    return lists, counts, owns, turns, bias


STEPS = (0, -1, 1, -2, 2, -3, 3, 4)


def shift(x, axis, by):
    n = lax.axis_size(axis)
    return lax.ppermute(x, axis, [(i, (i + by) % n) for i in range(n)])


def ring(kv):
    half = kv.shape[0] // 2
    up, down, held = kv, kv, [kv]
    for _ in range(3):
        up, down = shift(up, "z", 1), shift(down, "z", -1)
        held += [up, down]
    held += [shift(up[:half], "z", 1), shift(down[half:], "z", -1)]
    near, far = jnp.concatenate(held[:5]), jnp.concatenate(held[5:])
    return [near, far, shift(near, "core", 1), shift(far, "core", 1)]


def per_device(queries, keys, values, span_order, block_pattern, summary_flag):
    heads = keys.shape[1] // HEAD
    pieces = lax.axis_size("yhi")
    by_head = [x.reshape(SPAN, heads, HEAD).transpose(1, 0, 2) for x in (keys, values)]
    kv = jnp.concatenate(by_head, axis=2)
    kv = lax.all_to_all(kv, HEADS, split_axis=0, concat_axis=0, tiled=True)
    pieces_of_keys = ring(kv)

    order = span_order.reshape(2, 2, 2, lax.axis_size("z"), 2, 2)
    query_true = lax.dynamic_index_in_dim(order, lax.axis_index("z"), 3, keepdims=False)
    query_true = lax.dynamic_index_in_dim(query_true, lax.axis_index("core"), 1, keepdims=False)
    query_true = query_true.transpose(0, 1, 3, 2).reshape(-1)
    key_true = lax.dynamic_index_in_dim(order, lax.axis_index("yhi"), 4, keepdims=False)
    key_true = key_true.transpose(1, 3, 0, 2, 4)
    core, depth, z = lax.axis_index("core"), lax.axis_size("z"), lax.axis_index("z")
    key_true = jnp.take(key_true, (core + jnp.arange(2, dtype=jnp.int32)) % 2, axis=0)
    key_true = jnp.take(key_true, (z + jnp.array(STEPS, jnp.int32) + depth) % depth, axis=1).reshape(-1)

    q = queries.reshape(SPAN, heads, GROUP, HEAD).transpose(1, 2, 0, 3).reshape(heads, 1, ROWS, HEAD)
    q = jnp.broadcast_to(q, (heads, pieces, ROWS, HEAD)).reshape(heads * pieces, ROWS, HEAD)
    q = lax.all_to_all(q, HEADS + ("yhi",), split_axis=0, concat_axis=0, tiled=True)

    lists, counts, owns, turns, bias = tables(query_true, key_true, block_pattern, summary_flag)
    parts = attend(lists, counts, owns, turns, q, pieces_of_keys, bias)
    parts = lax.all_to_all(parts, HEADS + ("yhi",), split_axis=0, concat_axis=0, tiled=True)
    return combine(parts, pieces)


def solution(mesh):
    fine = Mesh(mesh.devices.reshape(2, 2, 2, 8, 2, 2), ALL)
    return jax.shard_map(
        per_device,
        mesh=fine,
        in_specs=(P(ALL, None), P(ALL, None), P(ALL, None), P(), P(), P()),
        out_specs=P(ALL, None),
        check_vma=False,
    )
```

profile of v0, /device:TPU:1, one launch (start us, length us, event | category | flops | bytes accessed | tf_op | source)
XLA Modules:
  0.0 102.1 jit_solution(13301619476151778072)
XLA Ops:
  0.0 0.9 copy-done
  0.9 0.9 bitcast_bitcast_fusion
  1.8 0.7 pad_maximum_fusion
  2.6 5.9 %all-to-all-start.1 = ((bf16[8,56,256]{2,1,0:T(8,128)(2,1)}), bf16[8,56,256]{2,1,0:T(8,128)(2,1)S(1)}, u32[]{:S(2)}, u32[]{:S(2)}) async-start(bf16[8,56,256]{2,1,0:T(8,128)(2,1)} %pad_maximum_fusion), calls=%async_computation.1 | async-start | bytes 458752 | tf_op jit(solution)/shard_map/all_to_all | solution.py:275
  9.1 0.6 gather_fusion
  9.8 0.6 gather_fusion.1
  10.7 1.5 %convert_reduce_fusion = (s32[16]{0:T(128)S(1)}, pred[16,128]{0,1:T(32,128)(4,1)S(1)}, s32[16]{0:T(128)}, pred[16,128]{0,1:T(8,128)(4,1)}) fusion(s32[16]{0:T(128)S(1)} %lt.94, s32[128]{0:T(128)S(1)} %select_n.106, s32[128]{0:T(128)S(1)} %iota_add_fusion, s32[256,256]{1,0:T(8,128)S(1)} %copy-done.15), kind=kOutput, calls=%fused_computation.18 | convolution fusion | flops 3268576 | bytes 267456 | tf_op jit(solution)/shard_map/dot_general | solution.py:29
  12.5 0.3 reshape.119
  13.0 1.0 select_reduce_fusion.refs_0_
  13.9 0.5 broadcast_compare_fusion
  14.5 1.1 %broadcast_in_dim.98 = bf16[8,2,224,128]{3,2,1,0:T(8,128)(2,1)} broadcast(bf16[8,224,128]{2,1,0:T(8,128)(2,1)S(1)} %bitcast.40), dimensions={0,2,3} | broadcast | bytes 1376256 | tf_op jit(solution)/shard_map/broadcast_in_dim | solution.py:289
  15.6 6.7 %all-to-all-start = ((bf16[16,224,128]{2,1,0:T(8,128)(2,1)}), bf16[16,224,128]{2,1,0:T(8,128)(2,1)S(1)}, u32[]{:S(2)}, u32[]{:S(2)}) async-start(bf16[16,224,128]{2,1,0:T(8,128)(2,1)} %bitcast.8), calls=%async_computation | async-start | bytes 1835008 | tf_op jit(solution)/shard_map/all_to_all | solution.py:290
  22.2 5.7 %collective-permute-start.1 = (bf16[8,56,256]{2,1,0:T(8,128)(2,1)S(1)}, bf16[8,56,256]{2,1,0:T(8,128)(2,1)S(1)}, u32[]{:S(2)}, u32[]{:S(2)}) collective-permute-start(bf16[8,56,256]{2,1,0:T(8,128)(2,1)S(1)} %all-to-all-done.1), channel_id=1, source_target_pairs={{0,28},{4,0},{8,4},{12,8},{16,12},{20,16},{24,20},{28,24},{1,29},{... | collective-permute-start | bytes 688136 | tf_op jit(solution)/shard_map/ppermute | solution.py:256
  28.1 3.2 %collective-permute-done.1 = bf16[8,56,256]{2,1,0:T(8,128)(2,1)S(1)} collective-permute-done((bf16[8,56,256]{2,1,0:T(8,128)(2,1)S(1)}, bf16[8,56,256]{2,1,0:T(8,128)(2,1)S(1)}, u32[]{:S(2)}, u32[]{:S(2)}) %collective-permute-start.1) | collective-permute-done | bytes 229408 | tf_op jit(solution)/shard_map/ppermute | solution.py:256
  31.3 3.4 %collective-permute-start.3 = (bf16[8,56,256]{2,1,0:T(8,128)(2,1)S(1)}, bf16[8,56,256]{2,1,0:T(8,128)(2,1)S(1)}, u32[]{:S(2)}, u32[]{:S(2)}) collective-permute-start(bf16[8,56,256]{2,1,0:T(8,128)(2,1)S(1)} %collective-permute-done.1), channel_id=1, source_target_pairs={{0,28},{4,0},{8,4},{12,8},{16,12},{20,16},{24,20},{28,24},{1,29},{... | collective-permute-start | bytes 688136 | tf_op jit(solution)/shard_map/ppermute | solution.py:256
  34.7 2.9 %collective-permute-done.3 = bf16[8,56,256]{2,1,0:T(8,128)(2,1)S(1)} collective-permute-done((bf16[8,56,256]{2,1,0:T(8,128)(2,1)S(1)}, bf16[8,56,256]{2,1,0:T(8,128)(2,1)S(1)}, u32[]{:S(2)}, u32[]{:S(2)}) %collective-permute-start.3) | collective-permute-done | bytes 229408 | tf_op jit(solution)/shard_map/ppermute | solution.py:256
  37.7 3.4 %collective-permute-start.5 = (bf16[8,56,256]{2,1,0:T(8,128)(2,1)S(1)}, bf16[8,56,256]{2,1,0:T(8,128)(2,1)S(1)}, u32[]{:S(2)}, u32[]{:S(2)}) collective-permute-start(bf16[8,56,256]{2,1,0:T(8,128)(2,1)S(1)} %collective-permute-done.3), channel_id=1, source_target_pairs={{0,28},{4,0},{8,4},{12,8},{16,12},{20,16},{24,20},{28,24},{1,29},{... | collective-permute-start | bytes 688136 | tf_op jit(solution)/shard_map/ppermute | solution.py:256
  41.2 3.7 %collective-permute-start.8 = (bf16[40,56,256]{2,1,0:T(8,128)(2,1)S(1)}, bf16[40,56,256]{2,1,0:T(8,128)(2,1)}, u32[]{:S(2)}, u32[]{:S(2)}) collective-permute-start(bf16[40,56,256]{2,1,0:T(8,128)(2,1)S(1)} %constant_dynamic-update-slice_fusion.refs_6_), channel_id=1, source_target_pairs={{0,64},{64,0},{1,65},{65,1},{2,66},{66,2},{3,67},{67,3},{4,68},{68... | collective-permute-start | bytes 3440648 | tf_op jit(solution)/shard_map/ppermute | solution.py:256
  44.8 3.0 %collective-permute-start.7 = (bf16[4,56,256]{2,1,0:T(8,128)(2,1)S(1)}, bf16[4,56,256]{2,1,0:T(8,128)(2,1)S(1)}, u32[]{:S(2)}, u32[]{:S(2)}) collective-permute-start(bf16[4,56,256]{2,1,0:T(8,128)(2,1)S(1)} %slice.13), channel_id=1, source_target_pairs={{0,28},{4,0},{8,4},{12,8},{16,12},{20,16},{24,20},{28,24},{1,29},{... | collective-permute-start | bytes 344072 | tf_op jit(solution)/shard_map/ppermute | solution.py:256
  48.0 4.8 %collective-permute-done.6 = bf16[4,56,256]{2,1,0:T(8,128)(2,1)S(1)} collective-permute-done((bf16[4,56,256]{2,1,0:T(8,128)(2,1)S(1)}, bf16[4,56,256]{2,1,0:T(8,128)(2,1)S(1)}, u32[]{:S(2)}, u32[]{:S(2)}) %collective-permute-start.6) | collective-permute-done | bytes 114720 | tf_op jit(solution)/shard_map/ppermute | solution.py:256
  52.9 5.3 %collective-permute-start.9 = (bf16[24,56,256]{2,1,0:T(8,128)(2,1)S(1)}, bf16[24,56,256]{2,1,0:T(8,128)(2,1)S(1)}, u32[]{:S(2)}, u32[]{:S(2)}) collective-permute-start(bf16[24,56,256]{2,1,0:T(8,128)(2,1)S(1)} %constant_dynamic-update-slice_fusion.5.refs_7_), channel_id=1, source_target_pairs={{0,64},{64,0},{1,65},{65,1},{2,66},{66,2},{3,67},{67,3},{4,68},{68... | collective-permute-start | bytes 2064392 | tf_op jit(solution)/shard_map/ppermute | solution.py:256
  58.2 0.7 select_reduce_fusion.2.refs_3_
  58.8 0.5 broadcast_add_fusion.refs_2_
  59.6 0.7 select_convert_fusion.refs_5_
  60.4 0.7 copy-done.1
  61.1 0.7 copy-done.2
  61.8 0.7 copy-done.4
  62.5 0.6 copy-done.5
  63.1 0.6 copy-done.6
  63.7 15.8 %shard_map.73 = bf16[16,240,128]{2,1,0:T(8,128)(2,1)S(1)} custom-call(s32[16,128]{1,0:T(8,128)S(1)} %copy-done.2, s32[16]{0:T(128)S(1)} %copy-done.4, s32[16]{0:T(128)S(1)} %copy-done.6, s32[16]{0:T(128)S(1)} %copy-done.5, bf16[16,224,128]{2,1,0:T(8,128)(2,1)S(1)} %all-to-all-done.refs_4_, bf16[128,16]{1,0:T(8,128)(2,1)S(1)} %copy-done.1, ...), custom_call_target="tpu_custom_call" | custom-call | tf_op jit(solution)/shard_map/pallas_call | solution.py:165
  79.5 21.2 %all_to_all.15.parts_ref = bf16[16,240,128]{2,1,0:T(8,128)(2,1)S(1)} all-to-all(bf16[16,240,128]{2,1,0:T(8,128)(2,1)S(1)} %shard_map.73), channel_id=1, replica_groups=mesh['xhi'=2,'core'=2,'xlo'=2,'z'=8,'yhi'=2,'ylo'=2] {'xhi','xlo','ylo',..., dimensions={0} | all-to-all | bytes 1966080 | tf_op jit(solution)/shard_map/all_to_all | solution.py:294
  100.7 1.4 %shard_map.74 = bf16[56,4096]{1,0:T(8,128)(2,1)} custom-call(bf16[16,240,128]{2,1,0:T(8,128)(2,1)S(1)} %all_to_all.15.parts_ref), custom_call_target="tpu_custom_call" | custom-call | tf_op jit(solution)/shard_map/pallas_call | solution.py:216
  (78 shorter events, 2.2 us)
Async XLA Ops:
  0.0 0.9 copy-start
  0.0 8.5 %copy-start.14 = (s32[8]{0:T(128)S(1)}, s32[8]{0:T(128)}, u32[]{:S(2)}) copy-start(s32[8]{0:T(128)} %constant.128.clone) | copy-start | bytes 100
  0.0 8.5 %copy-start.13 = (s32[256]{0:T(256)S(1)}, s32[256]{0:T(256)}, u32[]{:S(2)}) copy-start(s32[256]{0:T(256)} %param.10) | copy-start | bytes 3076
  0.0 10.7 %copy-start.15 = (s32[256,256]{1,0:T(8,128)S(1)}, s32[256,256]{1,0:T(8,128)}, u32[]{:S(2)}) copy-start(s32[256,256]{1,0:T(8,128)} %param.11) | copy-start | bytes 786436
  0.0 12.4 %copy-start.7 = (bf16[56,4096]{1,0:T(8,128)(2,1)S(1)}, bf16[56,4096]{1,0:T(8,128)(2,1)}, u32[]{:S(2)}) copy-start(bf16[56,4096]{1,0:T(8,128)(2,1)} %param.7) | copy-start | bytes 1376260
  2.6 11.9 %all-to-all-start.1 = ((bf16[8,56,256]{2,1,0:T(8,128)(2,1)}), bf16[8,56,256]{2,1,0:T(8,128)(2,1)S(1)}, u32[]{:S(2)}, u32[]{:S(2)}) async-start(bf16[8,56,256]{2,1,0:T(8,128)(2,1)} %pad_maximum_fusion), calls=%async_computation.1 | async-start | bytes 458752 | tf_op jit(solution)/shard_map/all_to_all | solution.py:275
  9.1 3.2 %copy-start.11 = (s32[16]{0:T(128)}, s32[16]{0:T(128)S(1)}, u32[]{:S(2)}) copy-start(s32[16]{0:T(128)S(1)} %lt.94) | copy-start | bytes 196
  10.7 1.6 %copy-start.9 = (s32[128]{0:T(128)}, s32[128]{0:T(128)S(1)}, u32[]{:S(2)}) copy-start(s32[128]{0:T(128)S(1)} %select_n.106) | copy-start | bytes 1540
  10.7 3.2 %copy-start.16 = (s32[256]{0:T(256)S(1)}, s32[256]{0:T(256)}, u32[]{:S(2)}) copy-start(s32[256]{0:T(256)} %param.12) | copy-start | bytes 3076
  12.2 15.7 %copy-start.3 = (s32[16]{0:T(128)}, s32[16]{0:T(128)S(1)}, u32[]{:S(2)}) copy-start(s32[16]{0:T(128)S(1)} %get-tuple-element.5.refs_1_) | copy-start | bytes 196
  15.6 44.8 %all-to-all-start = ((bf16[16,224,128]{2,1,0:T(8,128)(2,1)}), bf16[16,224,128]{2,1,0:T(8,128)(2,1)S(1)}, u32[]{:S(2)}, u32[]{:S(2)}) async-start(bf16[16,224,128]{2,1,0:T(8,128)(2,1)} %bitcast.8), calls=%async_computation | async-start | bytes 1835008 | tf_op jit(solution)/shard_map/all_to_all | solution.py:290
  22.2 9.0 %collective-permute-start.1 = (bf16[8,56,256]{2,1,0:T(8,128)(2,1)S(1)}, bf16[8,56,256]{2,1,0:T(8,128)(2,1)S(1)}, u32[]{:S(2)}, u32[]{:S(2)}) collective-permute-start(bf16[8,56,256]{2,1,0:T(8,128)(2,1)S(1)} %all-to-all-done.1), channel_id=1, source_target_pairs={{0,28},{4,0},{8,4},{12,8},{16,12},{20,16},{24,20},{28,24},{1,29},{... | collective-permute-start | bytes 688136 | tf_op jit(solution)/shard_map/ppermute | solution.py:256
  27.9 6.8 %collective-permute-start = (bf16[8,56,256]{2,1,0:T(8,128)(2,1)S(1)}, bf16[8,56,256]{2,1,0:T(8,128)(2,1)S(1)}, u32[]{:S(2)}, u32[]{:S(2)}) collective-permute-start(bf16[8,56,256]{2,1,0:T(8,128)(2,1)S(1)} %all-to-all-done.1), channel_id=1, source_target_pairs={{0,4},{4,8},{8,12},{12,16},{16,20},{20,24},{24,28},{28,0},{1,5},{5... | collective-permute-start | bytes 688136 | tf_op jit(solution)/shard_map/ppermute | solution.py:256
  31.3 6.4 %collective-permute-start.3 = (bf16[8,56,256]{2,1,0:T(8,128)(2,1)S(1)}, bf16[8,56,256]{2,1,0:T(8,128)(2,1)S(1)}, u32[]{:S(2)}, u32[]{:S(2)}) collective-permute-start(bf16[8,56,256]{2,1,0:T(8,128)(2,1)S(1)} %collective-permute-done.1), channel_id=1, source_target_pairs={{0,28},{4,0},{8,4},{12,8},{16,12},{20,16},{24,20},{28,24},{1,29},{... | collective-permute-start | bytes 688136 | tf_op jit(solution)/shard_map/ppermute | solution.py:256
  34.7 6.4 %collective-permute-start.2 = (bf16[8,56,256]{2,1,0:T(8,128)(2,1)S(1)}, bf16[8,56,256]{2,1,0:T(8,128)(2,1)S(1)}, u32[]{:S(2)}, u32[]{:S(2)}) collective-permute-start(bf16[8,56,256]{2,1,0:T(8,128)(2,1)S(1)} %collective-permute-done), channel_id=1, source_target_pairs={{0,4},{4,8},{8,12},{12,16},{16,20},{20,24},{24,28},{28,0},{1,5},{5... | collective-permute-start | bytes 688136 | tf_op jit(solution)/shard_map/ppermute | solution.py:256
  37.7 7.2 %collective-permute-start.5 = (bf16[8,56,256]{2,1,0:T(8,128)(2,1)S(1)}, bf16[8,56,256]{2,1,0:T(8,128)(2,1)S(1)}, u32[]{:S(2)}, u32[]{:S(2)}) collective-permute-start(bf16[8,56,256]{2,1,0:T(8,128)(2,1)S(1)} %collective-permute-done.3), channel_id=1, source_target_pairs={{0,28},{4,0},{8,4},{12,8},{16,12},{20,16},{24,20},{28,24},{1,29},{... | collective-permute-start | bytes 688136 | tf_op jit(solution)/shard_map/ppermute | solution.py:256
  41.1 6.8 %collective-permute-start.4 = (bf16[8,56,256]{2,1,0:T(8,128)(2,1)S(1)}, bf16[8,56,256]{2,1,0:T(8,128)(2,1)S(1)}, u32[]{:S(2)}, u32[]{:S(2)}) collective-permute-start(bf16[8,56,256]{2,1,0:T(8,128)(2,1)S(1)} %collective-permute-done.2), channel_id=1, source_target_pairs={{0,4},{4,8},{8,12},{12,16},{16,20},{20,24},{24,28},{28,0},{1,5},{5... | collective-permute-start | bytes 688136 | tf_op jit(solution)/shard_map/ppermute | solution.py:256
  41.1 17.7 %copy-start.17 = (pred[256]{0:T(512)(128)(4,1)S(1)}, pred[256]{0:T(512)(128)(4,1)}, u32[]{:S(2)}) copy-start(pred[256]{0:T(512)(128)(4,1)} %broadcast_compare_fusion) | copy-start | bytes 772
  41.1 17.7 %copy-start.18 = (s32[16]{0:T(128)S(1)}, s32[16]{0:T(128)}, u32[]{:S(2)}) copy-start(s32[16]{0:T(128)} %get-tuple-element.9) | copy-start | bytes 196
  41.1 18.3 %copy-start.10 = (s32[128]{0:T(128)S(1)}, s32[128]{0:T(128)}, u32[]{:S(2)}) copy-start(s32[128]{0:T(128)} %copy-done.9) | copy-start | bytes 1540
  41.1 18.5 %copy-start.8 = (pred[16,128]{0,1:T(8,128)(4,1)S(1)}, pred[16,128]{0,1:T(8,128)(4,1)}, u32[]{:S(2)}) copy-start(pred[16,128]{0,1:T(8,128)(4,1)} %get-tuple-element.10) | copy-start | bytes 6148
  41.1 18.5 %copy-start.12 = (s32[16]{0:T(128)S(1)}, s32[16]{0:T(128)}, u32[]{:S(2)}) copy-start(s32[16]{0:T(128)} %copy-done.11) | copy-start | bytes 196
  41.2 19.2 %collective-permute-start.8 = (bf16[40,56,256]{2,1,0:T(8,128)(2,1)S(1)}, bf16[40,56,256]{2,1,0:T(8,128)(2,1)}, u32[]{:S(2)}, u32[]{:S(2)}) collective-permute-start(bf16[40,56,256]{2,1,0:T(8,128)(2,1)S(1)} %constant_dynamic-update-slice_fusion.refs_6_), channel_id=1, source_target_pairs={{0,64},{64,0},{1,65},{65,1},{2,66},{66,2},{3,67},{67,3},{4,68},{68... | collective-permute-start | bytes 3440648 | tf_op jit(solution)/shard_map/ppermute | solution.py:256
  44.8 8.0 %collective-permute-start.7 = (bf16[4,56,256]{2,1,0:T(8,128)(2,1)S(1)}, bf16[4,56,256]{2,1,0:T(8,128)(2,1)S(1)}, u32[]{:S(2)}, u32[]{:S(2)}) collective-permute-start(bf16[4,56,256]{2,1,0:T(8,128)(2,1)S(1)} %slice.13), channel_id=1, source_target_pairs={{0,28},{4,0},{8,4},{12,8},{16,12},{20,16},{24,20},{28,24},{1,29},{... | collective-permute-start | bytes 344072 | tf_op jit(solution)/shard_map/ppermute | solution.py:256
  47.9 4.9 %collective-permute-start.6 = (bf16[4,56,256]{2,1,0:T(8,128)(2,1)S(1)}, bf16[4,56,256]{2,1,0:T(8,128)(2,1)S(1)}, u32[]{:S(2)}, u32[]{:S(2)}) collective-permute-start(bf16[4,56,256]{2,1,0:T(8,128)(2,1)S(1)} %slice.12), channel_id=1, source_target_pairs={{0,4},{4,8},{8,12},{12,16},{16,20},{20,24},{24,28},{28,0},{1,5},{5... | collective-permute-start | bytes 344072 | tf_op jit(solution)/shard_map/ppermute | solution.py:256
  52.9 7.5 %collective-permute-start.9 = (bf16[24,56,256]{2,1,0:T(8,128)(2,1)S(1)}, bf16[24,56,256]{2,1,0:T(8,128)(2,1)S(1)}, u32[]{:S(2)}, u32[]{:S(2)}) collective-permute-start(bf16[24,56,256]{2,1,0:T(8,128)(2,1)S(1)} %constant_dynamic-update-slice_fusion.5.refs_7_), channel_id=1, source_target_pairs={{0,64},{64,0},{1,65},{65,1},{2,66},{66,2},{3,67},{67,3},{4,68},{68... | collective-permute-start | bytes 2064392 | tf_op jit(solution)/shard_map/ppermute | solution.py:256
  60.3 0.8 copy-start.1
  61.1 0.7 copy-start.2
  61.8 0.7 copy-start.4
  62.5 0.6 copy-start.5
  63.1 0.6 copy-start.6
where the time goes:
time: 103 us; the launch traced here: 102 us
  starting transfers between devices  37.1 us (36%)
  blocking collectives  21.2 us (21%)
  Pallas kernels  17.2 us (17%)
  waiting for transfers between devices  10.9 us (11%)
  local copies, waits for them, and re-layouts  8.97 us (9%)
  other arithmetic  4.53 us (4%)
  matrix products  1.88 us (2%)
    ppermute x10, starting transfers between devices, shift(): return lax.ppermute(x, axis, [(i, (i + by) % n) for i in range(n)])  24.6 us
    all_to_all x1, blocking collectives, per_device(): lax.all_to_all(parts, HEADS + ('yhi',), split_axis=0, concat_axis=0, tile...  21.2 us
    pallas_call x1, Pallas kernels, attend(): pl.pallas_call(kernel, out_shape=jax.ShapeDtypeStruct((query_spans, ROWS...  15.8 us
    ppermute x10, waiting for transfers between devices, shift(): return lax.ppermute(x, axis, [(i, (i + by) % n) for i in range(n)])  10.9 us
    all_to_all x1, starting transfers between devices, per_device(): lax.all_to_all(q, HEADS + ('yhi',), split_axis=0, concat_axis=0, tiled=True)  6.68 us
    all_to_all x1, starting transfers between devices, per_device(): kv = lax.all_to_all(kv, HEADS, split_axis=0, concat_axis=0, tiled=True)  5.86 us
    unnamed x45, local copies, waits for them, and re-layouts  4.38 us
  transfers between devices with their start and end apart: 12, of which 3 were waited for; matrix products, arithmetic and copies ran while one was open for 8% of the time, Pallas kernels for 0%

commit v1 on v0

--- a/solution.py
+++ b/solution.py
@@ -30,11 +30,13 @@
 
 
 def attend_kernel(
-    list_ref, count_ref, own_ref, turn_ref, q_ref, bias_ref, *refs, pieces, together
+    table_ref, mask_ref, ours_ref, theirs_ref, *refs, pieces, together
 ):
     piece_refs, (out_ref, kv_ref, sums, base, held, turned) = refs[:pieces], refs[pieces:]
     key_spans = kv_ref.shape[0]
-    query_spans = q_ref.shape[0]
+    query_spans = out_ref.shape[0]
+    count_at, own_at, turn_at, side_at = range(key_spans, key_spans + 4)
+    side = table_ref[0, side_at]
 
     first = 0
     for piece_ref in piece_refs:
@@ -78,23 +80,25 @@
     key_lanes, value_lanes = pl.ds(0, HEAD), pl.ds(HEAD, HEAD)
 
     def some_spans(i, carry):
-        spans = [turn_ref[i * together + u] for u in range(together)]
-        counts = [count_ref[s] for s in spans]
-        owns = [own_ref[s] for s in spans]
+        spans = [table_ref[i * together + u, turn_at] for u in range(together)]
+        counts = [table_ref[s, count_at] for s in spans]
+        owns = [table_ref[s, own_at] for s in spans]
         most = counts[0]
         for c in counts[1:]:
             most = jnp.maximum(most, c)
         batches = (most + BATCH - 1) // BATCH
 
         for u, s in enumerate(spans):
-            turned[u] = q_ref[s].T
+            rows = jnp.where(s % 2 == side, ours_ref[s // 2], theirs_ref[s // 2]).astype(jnp.float32)
+            rows = jnp.concatenate([rows[:, g * HEAD : (g + 1) * HEAD] for g in range(GROUP)], axis=0)
+            turned[u] = rows.astype(jnp.bfloat16).T
 
         peaks = []
         for u, s in enumerate(spans):
             keys = jnp.concatenate([summary[:, :HEAD], pile([jnp.maximum(owns[u], 0)], key_lanes)], axis=0)
             scores = jnp.dot(keys, turned[u], preferred_element_type=jnp.float32) * SCORE_SCALE
-            here = (lax.broadcasted_iota(jnp.int32, (bias_ref.shape[1], ROWS), 0) == s).astype(jnp.bfloat16)
-            far = scores[:key_spans] + SUMMARY_BIAS + jnp.dot(bias_ref[...], here, preferred_element_type=jnp.float32)
+            here = (lax.broadcasted_iota(jnp.int32, (mask_ref.shape[1], ROWS), 0) == s).astype(jnp.bfloat16)
+            far = scores[:key_spans] + SUMMARY_BIAS + jnp.dot(mask_ref[...], here, preferred_element_type=jnp.float32)
             near = scores[key_spans : key_spans + SPAN] + (causal + jnp.where(owns[u] >= 0, 0.0, NEG))
             base[u, :key_spans] = far
             base[u, key_spans:] = near
@@ -103,7 +107,7 @@
         def score(t, peaks):
             new = []
             for u, s in enumerate(spans):
-                keys = pile([list_ref[s, t * BATCH + k] for k in range(BATCH)], key_lanes)
+                keys = pile([table_ref[s, t * BATCH + k] for k in range(BATCH)], key_lanes)
                 scores = jnp.dot(keys, turned[u], preferred_element_type=jnp.float32) * SCORE_SCALE
                 peak = peaks[u]
                 for k in range(BATCH):
@@ -128,7 +132,7 @@
             new = []
             for u, s in enumerate(spans):
                 total, mixed = state[u]
-                values = pile([list_ref[s, t * BATCH + k] for k in range(BATCH)], value_lanes)
+                values = pile([table_ref[s, t * BATCH + k] for k in range(BATCH)], value_lanes)
                 weight = jnp.exp2(held[u, t] - peaks[u])
                 total = total + add(weight)
                 parts = []
@@ -154,8 +158,8 @@
     lax.fori_loop(0, query_spans // together, some_spans, 0)
 
 
-def attend(lists, counts, owns, turns, q, pieces, bias):
-    query_spans, key_spans = q.shape[0], sum(piece.shape[0] for piece in pieces)
+def attend(table, mask, ours, theirs, pieces):
+    query_spans, key_spans = table.shape[0], sum(piece.shape[0] for piece in pieces)
     vmem = pl.BlockSpec(memory_space=pltpu.VMEM)
     smem = pl.BlockSpec(memory_space=pltpu.SMEM)
 
@@ -165,7 +169,7 @@
     return pl.pallas_call(
         kernel,
         out_shape=jax.ShapeDtypeStruct((query_spans, ROWS + EXTRA, HEAD), jnp.bfloat16),
-        in_specs=[smem] * 4 + [vmem] * (2 + len(pieces)),
+        in_specs=[smem] + [vmem] * (3 + len(pieces)),
         out_specs=vmem,
         scratch_shapes=[
             pltpu.VMEM((key_spans, SPAN, 2 * HEAD), jnp.bfloat16),
@@ -175,7 +179,7 @@
             pltpu.VMEM((TOGETHER, HEAD, ROWS), jnp.bfloat16),
         ],
         compiler_params=pltpu.CompilerParams(vmem_limit_bytes=48 * 1024 * 1024),
-    )(lists, counts, owns, turns, q, bias, *pieces)
+    )(table, mask, ours, theirs, *pieces)
 
 
 def combine_kernel(parts_ref, out_ref, *, pieces):
@@ -222,7 +226,7 @@
     )(parts)
 
 
-def tables(query_true, key_true, block_pattern, summary_flag):
+def tables(query_true, key_true, side, block_pattern, summary_flag):
     spans = block_pattern.shape[0]
     ids = jnp.arange(spans, dtype=jnp.int32)
     query_pick = (query_true[:, None] == ids[None, :]).astype(jnp.bfloat16)
@@ -245,9 +249,12 @@
     ahead = (counts[None, :] > counts[:, None]) | ((counts[None, :] == counts[:, None]) & (ids[None, :] < ids[:, None]))
     place = jnp.sum(ahead.astype(jnp.int32), axis=1, dtype=jnp.int32)
     turns = jnp.sum(jnp.where(place[None, :] == ids[:, None], ids[None, :], 0), axis=1, dtype=jnp.int32)
-    return lists, counts, owns, turns, bias
-
-
+    lane = jnp.arange(HEAD, dtype=jnp.int32)[None, :]
+    extra = jnp.where(lane == 0, counts[:, None], jnp.where(lane == 1, owns[:, None], jnp.where(lane == 2, turns[:, None], side)))
+    return jnp.concatenate([lists, extra], axis=1), bias
+
+
+TIE = 1
 STEPS = (0, -1, 1, -2, 2, -3, 3, 4)
 
 
@@ -256,24 +263,46 @@
     return lax.ppermute(x, axis, [(i, (i + by) % n) for i in range(n)])
 
 
-def ring(kv):
+def ring(kv, ours):
     half = kv.shape[0] // 2
     up, down, held = kv, kv, [kv]
-    for _ in range(3):
+    for step in range(3):
         up, down = shift(up, "z", 1), shift(down, "z", -1)
+        if step == 0:
+            theirs = shift(ours, "yhi", 1)
+        if step == TIE:
+            up, down, theirs = lax.optimization_barrier((up, down, theirs))
         held += [up, down]
     held += [shift(up[:half], "z", 1), shift(down[half:], "z", -1)]
     near, far = jnp.concatenate(held[:5]), jnp.concatenate(held[5:])
-    return [near, far, shift(near, "core", 1), shift(far, "core", 1)]
+    return [near, far, shift(near, "core", 1), shift(far, "core", 1)], theirs
+
+
+def pack_kernel(queries_ref, keys_ref, values_ref, out_ref):
+    wide = GROUP * HEAD
+    for h in range(out_ref.shape[0]):
+        out_ref[h, :, :wide] = queries_ref[:, h * wide : (h + 1) * wide]
+        out_ref[h, :, wide : wide + HEAD] = keys_ref[:, h * HEAD : (h + 1) * HEAD]
+        out_ref[h, :, wide + HEAD :] = values_ref[:, h * HEAD : (h + 1) * HEAD]
+
+
+def pack(queries, keys, values):
+    vmem = pl.BlockSpec(memory_space=pltpu.VMEM)
+    return pl.pallas_call(
+        pack_kernel,
+        out_shape=jax.ShapeDtypeStruct((keys.shape[1] // HEAD, SPAN, (GROUP + 2) * HEAD), jnp.bfloat16),
+        in_specs=[vmem] * 3,
+        out_specs=vmem,
+        compiler_params=pltpu.CompilerParams(vmem_limit_bytes=16 * 1024 * 1024),
+    )(queries, keys, values)
 
 
 def per_device(queries, keys, values, span_order, block_pattern, summary_flag):
     heads = keys.shape[1] // HEAD
     pieces = lax.axis_size("yhi")
-    by_head = [x.reshape(SPAN, heads, HEAD).transpose(1, 0, 2) for x in (keys, values)]
-    kv = jnp.concatenate(by_head, axis=2)
-    kv = lax.all_to_all(kv, HEADS, split_axis=0, concat_axis=0, tiled=True)
-    pieces_of_keys = ring(kv)
+    packed = pack(queries, keys, values)
+    packed = lax.all_to_all(packed, HEADS, split_axis=0, concat_axis=0, tiled=True)
+    ours, kv = packed[:, :, : GROUP * HEAD], packed[:, :, GROUP * HEAD :]
 
     order = span_order.reshape(2, 2, 2, lax.axis_size("z"), 2, 2)
     query_true = lax.dynamic_index_in_dim(order, lax.axis_index("z"), 3, keepdims=False)
@@ -284,13 +313,11 @@
     core, depth, z = lax.axis_index("core"), lax.axis_size("z"), lax.axis_index("z")
     key_true = jnp.take(key_true, (core + jnp.arange(2, dtype=jnp.int32)) % 2, axis=0)
     key_true = jnp.take(key_true, (z + jnp.array(STEPS, jnp.int32) + depth) % depth, axis=1).reshape(-1)
-
-    q = queries.reshape(SPAN, heads, GROUP, HEAD).transpose(1, 2, 0, 3).reshape(heads, 1, ROWS, HEAD)
-    q = jnp.broadcast_to(q, (heads, pieces, ROWS, HEAD)).reshape(heads * pieces, ROWS, HEAD)
-    q = lax.all_to_all(q, HEADS + ("yhi",), split_axis=0, concat_axis=0, tiled=True)
-
-    lists, counts, owns, turns, bias = tables(query_true, key_true, block_pattern, summary_flag)
-    parts = attend(lists, counts, owns, turns, q, pieces_of_keys, bias)
+    table, mask = tables(query_true, key_true, lax.axis_index("yhi"), block_pattern, summary_flag)
+
+    ours, kv, table, mask = lax.optimization_barrier((ours, kv, table, mask))
+    pieces_of_keys, theirs = ring(kv, ours)
+    parts = attend(table, mask, ours, theirs, pieces_of_keys)
     parts = lax.all_to_all(parts, HEADS + ("yhi",), split_axis=0, concat_axis=0, tiled=True)
     return combine(parts, pieces)
 

time: 103 us -> 94.2 us (0.915)
  waiting for transfers between devices: 10.9 us -> 17.4 us
  starting transfers between devices: 37.1 us -> 32.5 us
  local copies, waits for them, and re-layouts: 8.97 us -> 5.08 us
  other arithmetic: 4.53 us -> 1.1 us
  blocking collectives: 21.2 us -> 20 us
  matrix products: 1.88 us -> 0.76 us
    all_to_all x2 -> x1, waiting for transfers between devices: 0.01 us -> 6.58 us  [per_device(): lax.all_to_all(packed, HEADS, split_axis=0, concat_axis=0, tiled=True)]
    all_to_all x2 -> x1, starting transfers between devices: 12.5 us -> 5.99 us  [per_device(): lax.all_to_all(packed, HEADS, split_axis=0, concat_axis=0, tiled=True)]
    ppermute x10 -> x11, starting transfers between devices: 24.6 us -> 26.5 us  [shift(): return lax.ppermute(x, axis, [(i, (i + by) % n) for i in range(n)])]
    unnamed x45 -> x21, local copies, waits for them, and re-layouts: 4.38 us -> 2.95 us
    all_to_all x1, blocking collectives: 21.2 us -> 20 us  [per_device(): lax.all_to_all(parts, HEADS + ('yhi',), split_axis=0, concat_axis=0, tile...]
    transpose x2 -> x0, local copies, waits for them, and re-layouts: 1.12 us -> none  [the longest x1 0.94 us: per_device(): x.reshape(SPAN, heads, HEAD).transpose(1, 0, 2)]
    dot_general x2, matrix products: 1.68 us -> 0.56 us  [nt_dot(): lax.dot_general(a, b, (((1,), (1,)), ((), ())), preferred_element_type=jn...]
    pallas_call x1, Pallas kernels: 15.8 us -> 14.7 us  [attend(): pl.pallas_call(kernel, out_shape=jax.ShapeDtypeStruct((query_spans, ROWS...]
  transfers between devices with their start and end apart: 12 -> 12, of which waited for: 3 -> 6; matrix products, arithmetic and copies ran while one was open for 8% -> 4% of each run, Pallas kernels for 0% -> 0%
where the time goes in v1:
time: 94.2 us; the launch traced here: 94.1 us
  starting transfers between devices  32.5 us (35%)
  blocking collectives  20 us (21%)
  waiting for transfers between devices  17.4 us (18%)
  Pallas kernels  17 us (18%)
  local copies, waits for them, and re-layouts  5.08 us (5%)
  other arithmetic  1.1 us (1%)
    ppermute x11, starting transfers between devices, shift(): return lax.ppermute(x, axis, [(i, (i + by) % n) for i in range(n)])  26.5 us
    all_to_all x1, blocking collectives, per_device(): lax.all_to_all(parts, HEADS + ('yhi',), split_axis=0, concat_axis=0, tile...  20 us
    pallas_call x1, Pallas kernels, attend(): pl.pallas_call(kernel, out_shape=jax.ShapeDtypeStruct((query_spans, ROWS...  14.7 us
    ppermute x11, waiting for transfers between devices, shift(): return lax.ppermute(x, axis, [(i, (i + by) % n) for i in range(n)])  10.8 us
    all_to_all x1, waiting for transfers between devices, per_device(): lax.all_to_all(packed, HEADS, split_axis=0, concat_axis=0, tiled=True)  6.58 us
    all_to_all x1, starting transfers between devices, per_device(): lax.all_to_all(packed, HEADS, split_axis=0, concat_axis=0, tiled=True)  5.99 us
    unnamed x21, local copies, waits for them, and re-layouts  2.95 us
  transfers between devices with their start and end apart: 12, of which 6 were waited for; matrix products, arithmetic and copies ran while one was open for 4% of the time, Pallas kernels for 0%

profile of v1, /device:TPU:1, one launch (start us, length us, event | category | flops | bytes accessed | tf_op | source)
XLA Modules:
  0.0 94.1 jit_solution(14726521156999151061)
XLA Ops:
  0.0 1.0 %copy-done = bf16[56,4096]{1,0:T(8,128)(2,1)S(1)} copy-done((bf16[56,4096]{1,0:T(8,128)(2,1)S(1)}, bf16[56,4096]{1,0:T(8,128)(2,1)}, u32[]{:S(2)}) %copy-start) | copy-done | bytes 458776
  1.0 0.9 copy-done.1
  1.9 0.9 copy-done.2
  2.8 0.9 shard_map.73
  3.8 6.0 %all-to-all-start = ((bf16[8,56,768]{2,1,0:T(8,128)(2,1)}), bf16[8,56,768]{2,1,0:T(8,128)(2,1)S(1)}, u32[]{:S(2)}, u32[]{:S(2)}) async-start(bf16[8,56,768]{2,1,0:T(8,128)(2,1)} %shard_map.73), calls=%async_computation | async-start | bytes 1376256 | tf_op jit(solution)/shard_map/all_to_all | solution.py:304
  9.9 0.2 reshape.123
  10.4 0.6 gather_fusion
  11.1 0.1 copy.27
  11.2 0.6 gather_fusion.1
  11.9 0.1 select_n.117
  12.0 0.4 convert_reduce_fusion
  12.5 0.2 fusion
  12.7 0.2 convert_reduce_fusion.1
  13.1 0.4 select_reduce_fusion
  13.5 0.2 fusion.1
  13.7 0.1 select_convert_fusion.refs_1_
  13.8 6.6 %all-to-all-done = bf16[8,56,768]{2,1,0:T(8,128)(2,1)S(1)} async-done(((bf16[8,56,768]{2,1,0:T(8,128)(2,1)}), bf16[8,56,768]{2,1,0:T(8,128)(2,1)S(1)}, u32[]{:S(2)}, u32[]{:S(2)}) %all-to-all-start) | async-done | bytes 688160 | tf_op jit(solution)/shard_map/all_to_all | solution.py:304
  20.4 5.7 %collective-permute-start.2 = (bf16[8,56,256]{2,1,0:T(8,128)(2,1)S(1)}, bf16[8,56,256]{2,1,0:T(8,128)(2,1)S(1)}, u32[]{:S(2)}, u32[]{:S(2)}) collective-permute-start(bf16[8,56,256]{2,1,0:T(8,128)(2,1)S(1)} %slice.21), channel_id=1, source_target_pairs={{0,28},{4,0},{8,4},{12,8},{16,12},{20,16},{24,20},{28,24},{1,29},{... | collective-permute-start | bytes 688136 | tf_op jit(solution)/shard_map/ppermute | solution.py:263
  26.1 2.6 %collective-permute-start.4 = (bf16[8,56,512]{2,1,0:T(8,128)(2,1)S(1)}, bf16[8,56,512]{2,1,0:T(8,128)(2,1)S(1)}, u32[]{:S(2)}, u32[]{:S(2)}) collective-permute-start(bf16[8,56,512]{2,1,0:T(8,128)(2,1)S(1)} %slice.20.refs_2_), channel_id=1, source_target_pairs={{0,2},{2,0},{1,3},{3,1},{4,6},{6,4},{5,7},{7,5},{8,10},{10,8},{9,1... | collective-permute-start | bytes 1376264 | tf_op jit(solution)/shard_map/ppermute | solution.py:263
  28.7 0.7 collective-permute-done.2
  29.4 3.4 %collective-permute-start.3 = (bf16[8,56,256]{2,1,0:T(8,128)(2,1)S(1)}, bf16[8,56,256]{2,1,0:T(8,128)(2,1)S(1)}, u32[]{:S(2)}, u32[]{:S(2)}) collective-permute-start(bf16[8,56,256]{2,1,0:T(8,128)(2,1)S(1)} %collective-permute-done.2), channel_id=1, source_target_pairs={{0,28},{4,0},{8,4},{12,8},{16,12},{20,16},{24,20},{28,24},{1,29},{... | collective-permute-start | bytes 688136 | tf_op jit(solution)/shard_map/ppermute | solution.py:263
  32.9 4.9 %collective-permute-done.4.refs_3_ = bf16[8,56,512]{2,1,0:T(8,128)(2,1)S(1)} collective-permute-done((bf16[8,56,512]{2,1,0:T(8,128)(2,1)S(1)}, bf16[8,56,512]{2,1,0:T(8,128)(2,1)S(1)}, u32[]{:S(2)}, u32[]{:S(2)}) %collective-permute-start.4) | collective-permute-done | bytes 458784 | tf_op jit(solution)/shard_map/ppermute | solution.py:263
  37.8 1.4 %collective-permute-done.1 = bf16[8,56,256]{2,1,0:T(8,128)(2,1)S(1)} collective-permute-done((bf16[8,56,256]{2,1,0:T(8,128)(2,1)S(1)}, bf16[8,56,256]{2,1,0:T(8,128)(2,1)S(1)}, u32[]{:S(2)}, u32[]{:S(2)}) %collective-permute-start.1) | collective-permute-done | bytes 229408 | tf_op jit(solution)/shard_map/ppermute | solution.py:263
  39.2 2.7 %collective-permute-start.6 = (bf16[8,56,256]{2,1,0:T(8,128)(2,1)S(1)}, bf16[8,56,256]{2,1,0:T(8,128)(2,1)S(1)}, u32[]{:S(2)}, u32[]{:S(2)}) collective-permute-start(bf16[8,56,256]{2,1,0:T(8,128)(2,1)S(1)} %collective-permute-done.3), channel_id=1, source_target_pairs={{0,28},{4,0},{8,4},{12,8},{16,12},{20,16},{24,20},{28,24},{1,29},{... | collective-permute-start | bytes 688136 | tf_op jit(solution)/shard_map/ppermute | solution.py:263
  41.9 4.3 %collective-permute-start.9 = (bf16[40,56,256]{2,1,0:T(8,128)(2,1)S(1)}, bf16[40,56,256]{2,1,0:T(8,128)(2,1)S(1)}, u32[]{:S(2)}, u32[]{:S(2)}) collective-permute-start(bf16[40,56,256]{2,1,0:T(8,128)(2,1)S(1)} %constant_dynamic-update-slice_fusion.refs_4_), channel_id=1, source_target_pairs={{0,64},{64,0},{1,65},{65,1},{2,66},{66,2},{3,67},{67,3},{4,68},{68... | collective-permute-start | bytes 3440648 | tf_op jit(solution)/shard_map/ppermute | solution.py:263
  46.3 2.7 %collective-permute-start.8 = (bf16[4,56,256]{2,1,0:T(8,128)(2,1)S(1)}, bf16[4,56,256]{2,1,0:T(8,128)(2,1)S(1)}, u32[]{:S(2)}, u32[]{:S(2)}) collective-permute-start(bf16[4,56,256]{2,1,0:T(8,128)(2,1)S(1)} %slice.23), channel_id=1, source_target_pairs={{0,28},{4,0},{8,4},{12,8},{16,12},{20,16},{24,20},{28,24},{1,29},{... | collective-permute-start | bytes 344072 | tf_op jit(solution)/shard_map/ppermute | solution.py:263
  49.1 2.0 %collective-permute-done.7 = bf16[4,56,256]{2,1,0:T(8,128)(2,1)S(1)} collective-permute-done((bf16[4,56,256]{2,1,0:T(8,128)(2,1)S(1)}, bf16[4,56,256]{2,1,0:T(8,128)(2,1)S(1)}, u32[]{:S(2)}, u32[]{:S(2)}) %collective-permute-start.7) | collective-permute-done | bytes 114720 | tf_op jit(solution)/shard_map/ppermute | solution.py:263
  51.2 5.1 %collective-permute-start.10 = (bf16[24,56,256]{2,1,0:T(8,128)(2,1)S(1)}, bf16[24,56,256]{2,1,0:T(8,128)(2,1)S(1)}, u32[]{:S(2)}, u32[]{:S(2)}) collective-permute-start(bf16[24,56,256]{2,1,0:T(8,128)(2,1)S(1)} %constant_dynamic-update-slice_fusion.5.refs_5_), channel_id=1, source_target_pairs={{0,64},{64,0},{1,65},{65,1},{2,66},{66,2},{3,67},{67,3},{4,68},{68... | collective-permute-start | bytes 2064392 | tf_op jit(solution)/shard_map/ppermute | solution.py:263
  56.3 1.8 %collective-permute-done.10.refs_7_ = bf16[24,56,256]{2,1,0:T(8,128)(2,1)S(1)} collective-permute-done((bf16[24,56,256]{2,1,0:T(8,128)(2,1)S(1)}, bf16[24,56,256]{2,1,0:T(8,128)(2,1)S(1)}, u32[]{:S(2)}, u32[]{:S(2)}) %collective-permute-start.10) | collective-permute-done | bytes 688160 | tf_op jit(solution)/shard_map/ppermute | solution.py:263
  58.1 14.7 %shard_map.74 = bf16[16,240,128]{2,1,0:T(8,128)(2,1)S(1)} custom-call(s32[16,256]{1,0:T(8,128)S(1)} %pad_add_fusion.refs_0_, bf16[128,16]{1,0:T(8,128)(2,1)S(1)} %select_convert_fusion.refs_1_, bf16[8,56,512]{2,1,0:T(8,128)(2,1)S(1)} %slice.20.refs_2_, bf16[8,56,512]{2,1,0:T(8,128)(2,1)S(1)} %collective-permute-done.4.refs_3_, ...), custom_call_target="tpu_custom_call" | custom-call | tf_op jit(solution)/shard_map/pallas_call | solution.py:169
  72.7 20.0 %all_to_all.10.parts_ref = bf16[16,240,128]{2,1,0:T(8,128)(2,1)S(1)} all-to-all(bf16[16,240,128]{2,1,0:T(8,128)(2,1)S(1)} %shard_map.74), channel_id=1, replica_groups=mesh['xhi'=2,'core'=2,'xlo'=2,'z'=8,'yhi'=2,'ylo'=2] {'xhi','xlo','ylo',..., dimensions={0} | all-to-all | bytes 1966080 | tf_op jit(solution)/shard_map/all_to_all | solution.py:321
  92.7 1.4 %shard_map.75 = bf16[56,4096]{1,0:T(8,128)(2,1)} custom-call(bf16[16,240,128]{2,1,0:T(8,128)(2,1)S(1)} %all_to_all.10.parts_ref), custom_call_target="tpu_custom_call" | custom-call | tf_op jit(solution)/shard_map/pallas_call | solution.py:220
  (56 shorter events, 1.2 us)
Async XLA Ops:
  0.0 9.8 %copy-start.4 = (s32[8]{0:T(128)S(1)}, s32[8]{0:T(128)}, u32[]{:S(2)}) copy-start(s32[8]{0:T(128)} %constant.130.clone) | copy-start | bytes 100
  0.0 1.0 %copy-start = (bf16[56,4096]{1,0:T(8,128)(2,1)S(1)}, bf16[56,4096]{1,0:T(8,128)(2,1)}, u32[]{:S(2)}) copy-start(bf16[56,4096]{1,0:T(8,128)(2,1)} %queries_ref.1) | copy-start | bytes 1376260
  1.0 0.9 copy-start.1
  1.9 0.9 copy-start.2
  2.8 7.0 %copy-start.3 = (s32[256]{0:T(256)S(1)}, s32[256]{0:T(256)}, u32[]{:S(2)}) copy-start(s32[256]{0:T(256)} %param.10) | copy-start | bytes 3076
  3.8 8.3 %copy-start.5 = (s32[256,256]{1,0:T(8,128)S(1)}, s32[256,256]{1,0:T(8,128)}, u32[]{:S(2)}) copy-start(s32[256,256]{1,0:T(8,128)} %param.11) | copy-start | bytes 786436
  3.8 8.9 %copy-start.6 = (s32[256]{0:T(256)S(1)}, s32[256]{0:T(256)}, u32[]{:S(2)}) copy-start(s32[256]{0:T(256)} %param.12) | copy-start | bytes 3076
  3.8 16.6 %all-to-all-start = ((bf16[8,56,768]{2,1,0:T(8,128)(2,1)}), bf16[8,56,768]{2,1,0:T(8,128)(2,1)S(1)}, u32[]{:S(2)}, u32[]{:S(2)}) async-start(bf16[8,56,768]{2,1,0:T(8,128)(2,1)} %shard_map.73), calls=%async_computation | async-start | bytes 1376256 | tf_op jit(solution)/shard_map/all_to_all | solution.py:304
  20.4 9.0 %collective-permute-start.2 = (bf16[8,56,256]{2,1,0:T(8,128)(2,1)S(1)}, bf16[8,56,256]{2,1,0:T(8,128)(2,1)S(1)}, u32[]{:S(2)}, u32[]{:S(2)}) collective-permute-start(bf16[8,56,256]{2,1,0:T(8,128)(2,1)S(1)} %slice.21), channel_id=1, source_target_pairs={{0,28},{4,0},{8,4},{12,8},{16,12},{20,16},{24,20},{28,24},{1,29},{... | collective-permute-start | bytes 688136 | tf_op jit(solution)/shard_map/ppermute | solution.py:263
  26.1 6.7 %collective-permute-start = (bf16[8,56,256]{2,1,0:T(8,128)(2,1)S(1)}, bf16[8,56,256]{2,1,0:T(8,128)(2,1)S(1)}, u32[]{:S(2)}, u32[]{:S(2)}) collective-permute-start(bf16[8,56,256]{2,1,0:T(8,128)(2,1)S(1)} %slice.21), channel_id=1, source_target_pairs={{0,4},{4,8},{8,12},{12,16},{16,20},{20,24},{24,28},{28,0},{1,5},{5... | collective-permute-start | bytes 688136 | tf_op jit(solution)/shard_map/ppermute | solution.py:263
  26.1 11.7 %collective-permute-start.4 = (bf16[8,56,512]{2,1,0:T(8,128)(2,1)S(1)}, bf16[8,56,512]{2,1,0:T(8,128)(2,1)S(1)}, u32[]{:S(2)}, u32[]{:S(2)}) collective-permute-start(bf16[8,56,512]{2,1,0:T(8,128)(2,1)S(1)} %slice.20.refs_2_), channel_id=1, source_target_pairs={{0,2},{2,0},{1,3},{3,1},{4,6},{6,4},{5,7},{7,5},{8,10},{10,8},{9,1... | collective-permute-start | bytes 1376264 | tf_op jit(solution)/shard_map/ppermute | solution.py:263
  29.4 8.3 %collective-permute-start.3 = (bf16[8,56,256]{2,1,0:T(8,128)(2,1)S(1)}, bf16[8,56,256]{2,1,0:T(8,128)(2,1)S(1)}, u32[]{:S(2)}, u32[]{:S(2)}) collective-permute-start(bf16[8,56,256]{2,1,0:T(8,128)(2,1)S(1)} %collective-permute-done.2), channel_id=1, source_target_pairs={{0,28},{4,0},{8,4},{12,8},{16,12},{20,16},{24,20},{28,24},{1,29},{... | collective-permute-start | bytes 688136 | tf_op jit(solution)/shard_map/ppermute | solution.py:263
  32.8 6.4 %collective-permute-start.1 = (bf16[8,56,256]{2,1,0:T(8,128)(2,1)S(1)}, bf16[8,56,256]{2,1,0:T(8,128)(2,1)S(1)}, u32[]{:S(2)}, u32[]{:S(2)}) collective-permute-start(bf16[8,56,256]{2,1,0:T(8,128)(2,1)S(1)} %collective-permute-done), channel_id=1, source_target_pairs={{0,4},{4,8},{8,12},{12,16},{16,20},{20,24},{24,28},{28,0},{1,5},{5... | collective-permute-start | bytes 688136 | tf_op jit(solution)/shard_map/ppermute | solution.py:263
  39.2 7.0 %collective-permute-start.5 = (bf16[8,56,256]{2,1,0:T(8,128)(2,1)S(1)}, bf16[8,56,256]{2,1,0:T(8,128)(2,1)S(1)}, u32[]{:S(2)}, u32[]{:S(2)}) collective-permute-start(bf16[8,56,256]{2,1,0:T(8,128)(2,1)S(1)} %collective-permute-done.1), channel_id=1, source_target_pairs={{0,4},{4,8},{8,12},{12,16},{16,20},{20,24},{24,28},{28,0},{1,5},{5... | collective-permute-start | bytes 688136 | tf_op jit(solution)/shard_map/ppermute | solution.py:263
  39.2 7.1 %collective-permute-start.6 = (bf16[8,56,256]{2,1,0:T(8,128)(2,1)S(1)}, bf16[8,56,256]{2,1,0:T(8,128)(2,1)S(1)}, u32[]{:S(2)}, u32[]{:S(2)}) collective-permute-start(bf16[8,56,256]{2,1,0:T(8,128)(2,1)S(1)} %collective-permute-done.3), channel_id=1, source_target_pairs={{0,28},{4,0},{8,4},{12,8},{16,12},{20,16},{24,20},{28,24},{1,29},{... | collective-permute-start | bytes 688136 | tf_op jit(solution)/shard_map/ppermute | solution.py:263
  41.9 16.1 %collective-permute-start.9 = (bf16[40,56,256]{2,1,0:T(8,128)(2,1)S(1)}, bf16[40,56,256]{2,1,0:T(8,128)(2,1)S(1)}, u32[]{:S(2)}, u32[]{:S(2)}) collective-permute-start(bf16[40,56,256]{2,1,0:T(8,128)(2,1)S(1)} %constant_dynamic-update-slice_fusion.refs_4_), channel_id=1, source_target_pairs={{0,64},{64,0},{1,65},{65,1},{2,66},{66,2},{3,67},{67,3},{4,68},{68... | collective-permute-start | bytes 3440648 | tf_op jit(solution)/shard_map/ppermute | solution.py:263
  46.2 4.9 %collective-permute-start.7 = (bf16[4,56,256]{2,1,0:T(8,128)(2,1)S(1)}, bf16[4,56,256]{2,1,0:T(8,128)(2,1)S(1)}, u32[]{:S(2)}, u32[]{:S(2)}) collective-permute-start(bf16[4,56,256]{2,1,0:T(8,128)(2,1)S(1)} %slice.22), channel_id=1, source_target_pairs={{0,4},{4,8},{8,12},{12,16},{16,20},{20,24},{24,28},{28,0},{1,5},{5... | collective-permute-start | bytes 344072 | tf_op jit(solution)/shard_map/ppermute | solution.py:263
  46.3 4.8 %collective-permute-start.8 = (bf16[4,56,256]{2,1,0:T(8,128)(2,1)S(1)}, bf16[4,56,256]{2,1,0:T(8,128)(2,1)S(1)}, u32[]{:S(2)}, u32[]{:S(2)}) collective-permute-start(bf16[4,56,256]{2,1,0:T(8,128)(2,1)S(1)} %slice.23), channel_id=1, source_target_pairs={{0,28},{4,0},{8,4},{12,8},{16,12},{20,16},{24,20},{28,24},{1,29},{... | collective-permute-start | bytes 344072 | tf_op jit(solution)/shard_map/ppermute | solution.py:263
  51.2 6.9 %collective-permute-start.10 = (bf16[24,56,256]{2,1,0:T(8,128)(2,1)S(1)}, bf16[24,56,256]{2,1,0:T(8,128)(2,1)S(1)}, u32[]{:S(2)}, u32[]{:S(2)}) collective-permute-start(bf16[24,56,256]{2,1,0:T(8,128)(2,1)S(1)} %constant_dynamic-update-slice_fusion.5.refs_5_), channel_id=1, source_target_pairs={{0,64},{64,0},{1,65},{65,1},{2,66},{66,2},{3,67},{67,3},{4,68},{68... | collective-permute-start | bytes 2064392 | tf_op jit(solution)/shard_map/ppermute | solution.py:263

commit v2 on v1

--- a/solution.py
+++ b/solution.py
@@ -14,7 +14,7 @@
 PADDED = 64
 ROWS = GROUP * SPAN
 EXTRA = 16
-BATCH = 4
+BATCH = 8
 TOGETHER = 4
 NEG = -1e30
 LOG2E = math.log2(math.e)
@@ -51,6 +51,9 @@
         first += piece_ref.shape[0]
     summary = (sums[...] / math.sqrt(SPAN)).astype(jnp.bfloat16)
 
+    summary_keys = jnp.concatenate([summary[:, :HEAD], mask_ref[...]], axis=1)
+    none = jnp.zeros((PADDED, HEAD), jnp.bfloat16)
+    span_row = lax.broadcasted_iota(jnp.int32, (HEAD, ROWS), 0)
     gap = jnp.zeros((PADDED - SPAN, HEAD), jnp.bfloat16)
     blank = jnp.zeros((PADDED - SPAN, ROWS), jnp.float32)
     key = lax.broadcasted_iota(jnp.int32, (SPAN, ROWS), 0)
@@ -91,14 +94,14 @@
         for u, s in enumerate(spans):
             rows = jnp.where(s % 2 == side, ours_ref[s // 2], theirs_ref[s // 2]).astype(jnp.float32)
             rows = jnp.concatenate([rows[:, g * HEAD : (g + 1) * HEAD] for g in range(GROUP)], axis=0)
-            turned[u] = rows.astype(jnp.bfloat16).T
+            turned[u, :HEAD] = rows.astype(jnp.bfloat16).T
+            turned[u, HEAD:] = (span_row == s).astype(jnp.bfloat16)
 
         peaks = []
         for u, s in enumerate(spans):
-            keys = jnp.concatenate([summary[:, :HEAD], pile([jnp.maximum(owns[u], 0)], key_lanes)], axis=0)
+            keys = jnp.concatenate([summary_keys, jnp.concatenate([pile([jnp.maximum(owns[u], 0)], key_lanes), none], axis=1)], axis=0)
             scores = jnp.dot(keys, turned[u], preferred_element_type=jnp.float32) * SCORE_SCALE
-            here = (lax.broadcasted_iota(jnp.int32, (mask_ref.shape[1], ROWS), 0) == s).astype(jnp.bfloat16)
-            far = scores[:key_spans] + SUMMARY_BIAS + jnp.dot(mask_ref[...], here, preferred_element_type=jnp.float32)
+            far = scores[:key_spans] + SUMMARY_BIAS
             near = scores[key_spans : key_spans + SPAN] + (causal + jnp.where(owns[u] >= 0, 0.0, NEG))
             base[u, :key_spans] = far
             base[u, key_spans:] = near
@@ -108,7 +111,7 @@
             new = []
             for u, s in enumerate(spans):
                 keys = pile([table_ref[s, t * BATCH + k] for k in range(BATCH)], key_lanes)
-                scores = jnp.dot(keys, turned[u], preferred_element_type=jnp.float32) * SCORE_SCALE
+                scores = jnp.dot(keys, turned[u, :HEAD], preferred_element_type=jnp.float32) * SCORE_SCALE
                 peak = peaks[u]
                 for k in range(BATCH):
                     part = scores[k * PADDED : k * PADDED + SPAN]
@@ -145,7 +148,7 @@
         for u, s in enumerate(spans):
             total, mixed = state[u]
             total = jnp.sum(total, axis=0, keepdims=True)
-            out_ref[s, :ROWS, :] = nt_dot(eye, (mixed / total).astype(jnp.bfloat16)).astype(jnp.bfloat16)
+            out_ref[s, :ROWS, :] = (mixed / total).astype(jnp.bfloat16).T
             level = peaks[u] + jnp.log2(total)
             first = level.astype(jnp.bfloat16).astype(jnp.float32)
             second = (level - first).astype(jnp.bfloat16).astype(jnp.float32)
@@ -176,7 +179,7 @@
             pltpu.VMEM((key_spans, 2 * HEAD), jnp.float32),
             pltpu.VMEM((TOGETHER, key_spans + SPAN, ROWS), jnp.float32),
             pltpu.VMEM((TOGETHER, key_spans // BATCH, BATCH * SPAN, ROWS), jnp.float32),
-            pltpu.VMEM((TOGETHER, HEAD, ROWS), jnp.bfloat16),
+            pltpu.VMEM((TOGETHER, 2 * HEAD, ROWS), jnp.bfloat16),
         ],
         compiler_params=pltpu.CompilerParams(vmem_limit_bytes=48 * 1024 * 1024),
     )(table, mask, ours, theirs, *pieces)
@@ -251,6 +254,7 @@
     turns = jnp.sum(jnp.where(place[None, :] == ids[:, None], ids[None, :], 0), axis=1, dtype=jnp.int32)
     lane = jnp.arange(HEAD, dtype=jnp.int32)[None, :]
     extra = jnp.where(lane == 0, counts[:, None], jnp.where(lane == 1, owns[:, None], jnp.where(lane == 2, turns[:, None], side)))
+    bias = jnp.concatenate([bias, jnp.zeros((bias.shape[0], HEAD - bias.shape[1]), jnp.bfloat16)], axis=1)
     return jnp.concatenate([lists, extra], axis=1), bias
 
 
@@ -273,27 +277,40 @@
         if step == TIE:
             up, down, theirs = lax.optimization_barrier((up, down, theirs))
         held += [up, down]
-    held += [shift(up[:half], "z", 1), shift(down[half:], "z", -1)]
+        if step == 1:
+            far_up, far_down = up[:half], down[half:]
+    held += [shift(far_up, "z", 2), shift(far_down, "z", -2)]
     near, far = jnp.concatenate(held[:5]), jnp.concatenate(held[5:])
     return [near, far, shift(near, "core", 1), shift(far, "core", 1)], theirs
 
 
-def pack_kernel(queries_ref, keys_ref, values_ref, out_ref):
+def pack_kernel(queries_ref, keys_ref, values_ref, out_ref, queries, keys, values, done):
     wide = GROUP * HEAD
+    copies = [
+        pltpu.make_async_copy(keys_ref, keys, done.at[0]),
+        pltpu.make_async_copy(values_ref, values, done.at[1]),
+        pltpu.make_async_copy(queries_ref, queries, done.at[2]),
+    ]
+    for copy in copies:
+        copy.start()
+    for copy in copies:
+        copy.wait()
     for h in range(out_ref.shape[0]):
-        out_ref[h, :, :wide] = queries_ref[:, h * wide : (h + 1) * wide]
-        out_ref[h, :, wide : wide + HEAD] = keys_ref[:, h * HEAD : (h + 1) * HEAD]
-        out_ref[h, :, wide + HEAD :] = values_ref[:, h * HEAD : (h + 1) * HEAD]
+        out_ref[h, :, :wide] = queries[:, h * wide : (h + 1) * wide]
+        out_ref[h, :, wide : wide + HEAD] = keys[:, h * HEAD : (h + 1) * HEAD]
+        out_ref[h, :, wide + HEAD :] = values[:, h * HEAD : (h + 1) * HEAD]
 
 
 def pack(queries, keys, values):
-    vmem = pl.BlockSpec(memory_space=pltpu.VMEM)
+    heads = keys.shape[1] // HEAD
     return pl.pallas_call(
         pack_kernel,
-        out_shape=jax.ShapeDtypeStruct((keys.shape[1] // HEAD, SPAN, (GROUP + 2) * HEAD), jnp.bfloat16),
-        in_specs=[vmem] * 3,
-        out_specs=vmem,
-        compiler_params=pltpu.CompilerParams(vmem_limit_bytes=16 * 1024 * 1024),
+        out_shape=jax.ShapeDtypeStruct((heads, SPAN, (GROUP + 2) * HEAD), jnp.bfloat16),
+        in_specs=[pl.BlockSpec(memory_space=pl.ANY)] * 3,
+        out_specs=pl.BlockSpec(memory_space=pltpu.VMEM),
+        scratch_shapes=[pltpu.VMEM(x.shape, x.dtype) for x in (queries, keys, values)]
+        + [pltpu.SemaphoreType.DMA((3,))],
+        compiler_params=pltpu.CompilerParams(vmem_limit_bytes=60 * 1024 * 1024),
     )(queries, keys, values)
 
 

time: 94.2 us -> 90.4 us (0.960)
  the two profiles are of different devices: /device:TPU:1 before, /device:TPU:32 now
where the time goes in v2:
time: 90.4 us; the launch traced here: 90.7 us
  waiting for transfers between devices  26.6 us (29%)
  blocking collectives  23.7 us (26%)
  starting transfers between devices  20.3 us (22%)
  Pallas kernels  15.7 us (17%)
  local copies, waits for them, and re-layouts  2.26 us (2%)
  other arithmetic  1.09 us (1%)
    all_to_all x1, blocking collectives, per_device(): lax.all_to_all(parts, HEADS + ('yhi',), split_axis=0, concat_axis=0, tile...  23.7 us
    ppermute x11, waiting for transfers between devices, shift(): return lax.ppermute(x, axis, [(i, (i + by) % n) for i in range(n)])  19.5 us
    ppermute x11, starting transfers between devices, shift(): return lax.ppermute(x, axis, [(i, (i + by) % n) for i in range(n)])  14.8 us
    pallas_call x1, Pallas kernels, attend(): pl.pallas_call(kernel, out_shape=jax.ShapeDtypeStruct((query_spans, ROWS...  12.1 us
    all_to_all x1, waiting for transfers between devices, per_device(): lax.all_to_all(packed, HEADS, split_axis=0, concat_axis=0, tiled=True)  7.17 us
    all_to_all x1, starting transfers between devices, per_device(): lax.all_to_all(packed, HEADS, split_axis=0, concat_axis=0, tiled=True)  5.46 us
    pallas_call x1, Pallas kernels, pack(): pl.pallas_call(pack_kernel, out_shape=jax.ShapeDtypeStruct((heads, SPAN,...  2.1 us
  transfers between devices with their start and end apart: 12, of which 8 were waited for; matrix products, arithmetic and copies ran while one was open for 4% of the time, Pallas kernels for 0%

profile of v2, /device:TPU:32, one launch (start us, length us, event | category | flops | bytes accessed | tf_op | source)
XLA Modules:
  0.0 90.7 jit_solution(15201720838793409093)
XLA Ops:
  0.0 2.1 %shard_map.73 = bf16[8,56,768]{2,1,0:T(8,128)(2,1)} custom-call(bf16[56,4096]{1,0:T(8,128)(2,1)} %queries_ref.1, bf16[56,1024]{1,0:T(8,128)(2,1)} %keys_ref.1, bf16[56,1024]{1,0:T(8,128)(2,1)} %values_ref.1), custom_call_target="tpu_custom_call" | custom-call | tf_op jit(solution)/shard_map/pallas_call | solution.py:306
  2.1 5.5 %all-to-all-start = ((bf16[8,56,768]{2,1,0:T(8,128)(2,1)}), bf16[8,56,768]{2,1,0:T(8,128)(2,1)S(1)}, u32[]{:S(2)}, u32[]{:S(2)}) async-start(bf16[8,56,768]{2,1,0:T(8,128)(2,1)} %shard_map.73), calls=%async_computation | async-start | bytes 1376256 | tf_op jit(solution)/shard_map/all_to_all | solution.py:321
  7.7 0.2 reshape.123
  7.9 0.1 copy.26
  8.2 0.6 gather_fusion
  8.9 0.1 copy.27
  9.0 0.6 gather_fusion.1
  9.7 0.1 select_n.117
  9.9 0.4 convert_reduce_fusion
  10.3 0.2 fusion
  10.5 0.2 fusion.1
  10.7 0.2 convert_reduce_fusion.1
  10.9 0.1 select_reduce_fusion.2
  11.1 0.4 select_reduce_fusion
  11.7 7.2 %all-to-all-done = bf16[8,56,768]{2,1,0:T(8,128)(2,1)S(1)} async-done(((bf16[8,56,768]{2,1,0:T(8,128)(2,1)}), bf16[8,56,768]{2,1,0:T(8,128)(2,1)S(1)}, u32[]{:S(2)}, u32[]{:S(2)}) %all-to-all-start) | async-done | bytes 688160 | tf_op jit(solution)/shard_map/all_to_all | solution.py:321
  18.9 0.2 collective-permute-start.2
  19.1 1.9 %collective-permute-start = (bf16[8,56,256]{2,1,0:T(8,128)(2,1)S(1)}, bf16[8,56,256]{2,1,0:T(8,128)(2,1)S(1)}, u32[]{:S(2)}, u32[]{:S(2)}) collective-permute-start(bf16[8,56,256]{2,1,0:T(8,128)(2,1)S(1)} %slice.21), channel_id=1, source_target_pairs={{0,4},{4,8},{8,12},{12,16},{16,20},{20,24},{24,28},{28,0},{1,5},{5... | collective-permute-start | bytes 688136 | tf_op jit(solution)/shard_map/ppermute | solution.py:267
  21.0 2.9 %collective-permute-start.4 = (bf16[8,56,512]{2,1,0:T(8,128)(2,1)S(1)}, bf16[8,56,512]{2,1,0:T(8,128)(2,1)S(1)}, u32[]{:S(2)}, u32[]{:S(2)}) collective-permute-start(bf16[8,56,512]{2,1,0:T(8,128)(2,1)S(1)} %slice.20.refs_2_), channel_id=1, source_target_pairs={{0,2},{2,0},{1,3},{3,1},{4,6},{6,4},{5,7},{7,5},{8,10},{10,8},{9,1... | collective-permute-start | bytes 1376264 | tf_op jit(solution)/shard_map/ppermute | solution.py:267
  23.9 1.7 %collective-permute-done.2 = bf16[8,56,256]{2,1,0:T(8,128)(2,1)S(1)} collective-permute-done((bf16[8,56,256]{2,1,0:T(8,128)(2,1)S(1)}, bf16[8,56,256]{2,1,0:T(8,128)(2,1)S(1)}, u32[]{:S(2)}, u32[]{:S(2)}) %collective-permute-start.2) | collective-permute-done | bytes 229408 | tf_op jit(solution)/shard_map/ppermute | solution.py:267
  25.6 3.3 %collective-permute-start.3 = (bf16[8,56,256]{2,1,0:T(8,128)(2,1)S(1)}, bf16[8,56,256]{2,1,0:T(8,128)(2,1)S(1)}, u32[]{:S(2)}, u32[]{:S(2)}) collective-permute-start(bf16[8,56,256]{2,1,0:T(8,128)(2,1)S(1)} %collective-permute-done.2), channel_id=1, source_target_pairs={{0,28},{4,0},{8,4},{12,8},{16,12},{20,16},{24,20},{28,24},{1,29},{... | collective-permute-start | bytes 688136 | tf_op jit(solution)/shard_map/ppermute | solution.py:267
  28.9 0.5 collective-permute-done
  29.4 4.2 %collective-permute-done.4.refs_3_ = bf16[8,56,512]{2,1,0:T(8,128)(2,1)S(1)} collective-permute-done((bf16[8,56,512]{2,1,0:T(8,128)(2,1)S(1)}, bf16[8,56,512]{2,1,0:T(8,128)(2,1)S(1)}, u32[]{:S(2)}, u32[]{:S(2)}) %collective-permute-start.4) | collective-permute-done | bytes 458784 | tf_op jit(solution)/shard_map/ppermute | solution.py:267
  33.6 3.0 %collective-permute-done.1 = bf16[8,56,256]{2,1,0:T(8,128)(2,1)S(1)} collective-permute-done((bf16[8,56,256]{2,1,0:T(8,128)(2,1)S(1)}, bf16[8,56,256]{2,1,0:T(8,128)(2,1)S(1)}, u32[]{:S(2)}, u32[]{:S(2)}) %collective-permute-start.1) | collective-permute-done | bytes 229408 | tf_op jit(solution)/shard_map/ppermute | solution.py:267
  36.7 3.3 %collective-permute-start.6 = (bf16[8,56,256]{2,1,0:T(8,128)(2,1)S(1)}, bf16[8,56,256]{2,1,0:T(8,128)(2,1)S(1)}, u32[]{:S(2)}, u32[]{:S(2)}) collective-permute-start(bf16[8,56,256]{2,1,0:T(8,128)(2,1)S(1)} %collective-permute-done.3), channel_id=1, source_target_pairs={{0,28},{4,0},{8,4},{12,8},{16,12},{20,16},{24,20},{28,24},{1,29},{... | collective-permute-start | bytes 688136 | tf_op jit(solution)/shard_map/ppermute | solution.py:267
  40.0 2.7 %collective-permute-start.8 = (bf16[4,56,256]{2,1,0:T(8,128)(2,1)S(1)}, bf16[4,56,256]{2,1,0:T(8,128)(2,1)S(1)}, u32[]{:S(2)}, u32[]{:S(2)}) collective-permute-start(bf16[4,56,256]{2,1,0:T(8,128)(2,1)S(1)} %slice.15), channel_id=1, source_target_pairs={{0,24},{4,28},{8,0},{12,4},{16,8},{20,12},{24,16},{28,20},{1,25},{... | collective-permute-start | bytes 344072 | tf_op jit(solution)/shard_map/ppermute | solution.py:267
  42.8 0.2 collective-permute-start.7
  43.1 2.6 %collective-permute-done.5 = bf16[8,56,256]{2,1,0:T(8,128)(2,1)S(1)} collective-permute-done((bf16[8,56,256]{2,1,0:T(8,128)(2,1)S(1)}, bf16[8,56,256]{2,1,0:T(8,128)(2,1)S(1)}, u32[]{:S(2)}, u32[]{:S(2)}) %collective-permute-start.5) | collective-permute-done | bytes 229408 | tf_op jit(solution)/shard_map/ppermute | solution.py:267
  45.8 5.3 %collective-permute-done.7 = bf16[4,56,256]{2,1,0:T(8,128)(2,1)S(1)} collective-permute-done((bf16[4,56,256]{2,1,0:T(8,128)(2,1)S(1)}, bf16[4,56,256]{2,1,0:T(8,128)(2,1)S(1)}, u32[]{:S(2)}, u32[]{:S(2)}) %collective-permute-start.7) | collective-permute-done | bytes 114720 | tf_op jit(solution)/shard_map/ppermute | solution.py:267
  51.3 2.1 %collective-permute-done.10.refs_7_ = bf16[24,56,256]{2,1,0:T(8,128)(2,1)S(1)} collective-permute-done((bf16[24,56,256]{2,1,0:T(8,128)(2,1)S(1)}, bf16[24,56,256]{2,1,0:T(8,128)(2,1)S(1)}, u32[]{:S(2)}, u32[]{:S(2)}) %collective-permute-start.10) | collective-permute-done | bytes 688160 | tf_op jit(solution)/shard_map/ppermute | solution.py:267
  53.4 12.1 %shard_map.74 = bf16[16,240,128]{2,1,0:T(8,128)(2,1)S(1)} custom-call(s32[16,256]{1,0:T(8,128)S(1)} %pad_add_fusion.refs_0_, bf16[128,128]{1,0:T(8,128)(2,1)S(1)} %concatenate.13.refs_1_, bf16[8,56,512]{2,1,0:T(8,128)(2,1)S(1)} %slice.20.refs_2_, bf16[8,56,512]{2,1,0:T(8,128)(2,1)S(1)} %collective-permute-done.4.refs_3_, ...), custom_call_target="tpu_custom_call" | custom-call | tf_op jit(solution)/shard_map/pallas_call | solution.py:172
  65.6 23.7 %all_to_all.10.parts_ref = bf16[16,240,128]{2,1,0:T(8,128)(2,1)S(1)} all-to-all(bf16[16,240,128]{2,1,0:T(8,128)(2,1)S(1)} %shard_map.74), channel_id=1, replica_groups=mesh['xhi'=2,'core'=2,'xlo'=2,'z'=8,'yhi'=2,'ylo'=2] {'xhi','xlo','ylo',..., dimensions={0} | all-to-all | bytes 1966080 | tf_op jit(solution)/shard_map/all_to_all | solution.py:338
  89.3 1.4 %shard_map.75 = bf16[56,4096]{1,0:T(8,128)(2,1)} custom-call(bf16[16,240,128]{2,1,0:T(8,128)(2,1)S(1)} %all_to_all.10.parts_ref), custom_call_target="tpu_custom_call" | custom-call | tf_op jit(solution)/shard_map/pallas_call | solution.py:223
  (51 shorter events, 1.2 us)
Async XLA Ops:
  0.0 7.7 %copy-start.1 = (s32[8]{0:T(128)S(1)}, s32[8]{0:T(128)}, u32[]{:S(2)}) copy-start(s32[8]{0:T(128)} %constant.132.clone) | copy-start | bytes 100
  0.0 7.7 %copy-start = (s32[256]{0:T(256)S(1)}, s32[256]{0:T(256)}, u32[]{:S(2)}) copy-start(s32[256]{0:T(256)} %param.10) | copy-start | bytes 3076
  2.1 7.8 %copy-start.2 = (s32[256,256]{1,0:T(8,128)S(1)}, s32[256,256]{1,0:T(8,128)}, u32[]{:S(2)}) copy-start(s32[256,256]{1,0:T(8,128)} %param.11) | copy-start | bytes 786436
  2.1 8.4 %copy-start.3 = (s32[256]{0:T(256)S(1)}, s32[256]{0:T(256)}, u32[]{:S(2)}) copy-start(s32[256]{0:T(256)} %param.12) | copy-start | bytes 3076
  2.1 16.7 %all-to-all-start = ((bf16[8,56,768]{2,1,0:T(8,128)(2,1)}), bf16[8,56,768]{2,1,0:T(8,128)(2,1)S(1)}, u32[]{:S(2)}, u32[]{:S(2)}) async-start(bf16[8,56,768]{2,1,0:T(8,128)(2,1)} %shard_map.73), calls=%async_computation | async-start | bytes 1376256 | tf_op jit(solution)/shard_map/all_to_all | solution.py:321
  18.9 6.7 %collective-permute-start.2 = (bf16[8,56,256]{2,1,0:T(8,128)(2,1)S(1)}, bf16[8,56,256]{2,1,0:T(8,128)(2,1)S(1)}, u32[]{:S(2)}, u32[]{:S(2)}) collective-permute-start(bf16[8,56,256]{2,1,0:T(8,128)(2,1)S(1)} %slice.21), channel_id=1, source_target_pairs={{0,28},{4,0},{8,4},{12,8},{16,12},{20,16},{24,20},{28,24},{1,29},{... | collective-permute-start | bytes 688136 | tf_op jit(solution)/shard_map/ppermute | solution.py:267
  19.1 10.3 %collective-permute-start = (bf16[8,56,256]{2,1,0:T(8,128)(2,1)S(1)}, bf16[8,56,256]{2,1,0:T(8,128)(2,1)S(1)}, u32[]{:S(2)}, u32[]{:S(2)}) collective-permute-start(bf16[8,56,256]{2,1,0:T(8,128)(2,1)S(1)} %slice.21), channel_id=1, source_target_pairs={{0,4},{4,8},{8,12},{12,16},{16,20},{20,24},{24,28},{28,0},{1,5},{5... | collective-permute-start | bytes 688136 | tf_op jit(solution)/shard_map/ppermute | solution.py:267
  21.0 12.6 %collective-permute-start.4 = (bf16[8,56,512]{2,1,0:T(8,128)(2,1)S(1)}, bf16[8,56,512]{2,1,0:T(8,128)(2,1)S(1)}, u32[]{:S(2)}, u32[]{:S(2)}) collective-permute-start(bf16[8,56,512]{2,1,0:T(8,128)(2,1)S(1)} %slice.20.refs_2_), channel_id=1, source_target_pairs={{0,2},{2,0},{1,3},{3,1},{4,6},{6,4},{5,7},{7,5},{8,10},{10,8},{9,1... | collective-permute-start | bytes 1376264 | tf_op jit(solution)/shard_map/ppermute | solution.py:267
  25.6 8.0 %collective-permute-start.3 = (bf16[8,56,256]{2,1,0:T(8,128)(2,1)S(1)}, bf16[8,56,256]{2,1,0:T(8,128)(2,1)S(1)}, u32[]{:S(2)}, u32[]{:S(2)}) collective-permute-start(bf16[8,56,256]{2,1,0:T(8,128)(2,1)S(1)} %collective-permute-done.2), channel_id=1, source_target_pairs={{0,28},{4,0},{8,4},{12,8},{16,12},{20,16},{24,20},{28,24},{1,29},{... | collective-permute-start | bytes 688136 | tf_op jit(solution)/shard_map/ppermute | solution.py:267
  29.4 7.2 %collective-permute-start.1 = (bf16[8,56,256]{2,1,0:T(8,128)(2,1)S(1)}, bf16[8,56,256]{2,1,0:T(8,128)(2,1)S(1)}, u32[]{:S(2)}, u32[]{:S(2)}) collective-permute-start(bf16[8,56,256]{2,1,0:T(8,128)(2,1)S(1)} %collective-permute-done), channel_id=1, source_target_pairs={{0,4},{4,8},{8,12},{12,16},{16,20},{20,24},{24,28},{28,0},{1,5},{5... | collective-permute-start | bytes 688136 | tf_op jit(solution)/shard_map/ppermute | solution.py:267
  36.6 9.1 %collective-permute-start.5 = (bf16[8,56,256]{2,1,0:T(8,128)(2,1)S(1)}, bf16[8,56,256]{2,1,0:T(8,128)(2,1)S(1)}, u32[]{:S(2)}, u32[]{:S(2)}) collective-permute-start(bf16[8,56,256]{2,1,0:T(8,128)(2,1)S(1)} %collective-permute-done.1), channel_id=1, source_target_pairs={{0,4},{4,8},{8,12},{12,16},{16,20},{20,24},{24,28},{28,0},{1,5},{5... | collective-permute-start | bytes 688136 | tf_op jit(solution)/shard_map/ppermute | solution.py:267
  36.7 9.0 %collective-permute-start.6 = (bf16[8,56,256]{2,1,0:T(8,128)(2,1)S(1)}, bf16[8,56,256]{2,1,0:T(8,128)(2,1)S(1)}, u32[]{:S(2)}, u32[]{:S(2)}) collective-permute-start(bf16[8,56,256]{2,1,0:T(8,128)(2,1)S(1)} %collective-permute-done.3), channel_id=1, source_target_pairs={{0,28},{4,0},{8,4},{12,8},{16,12},{20,16},{24,20},{28,24},{1,29},{... | collective-permute-start | bytes 688136 | tf_op jit(solution)/shard_map/ppermute | solution.py:267
  40.0 11.1 %collective-permute-start.8 = (bf16[4,56,256]{2,1,0:T(8,128)(2,1)S(1)}, bf16[4,56,256]{2,1,0:T(8,128)(2,1)S(1)}, u32[]{:S(2)}, u32[]{:S(2)}) collective-permute-start(bf16[4,56,256]{2,1,0:T(8,128)(2,1)S(1)} %slice.15), channel_id=1, source_target_pairs={{0,24},{4,28},{8,0},{12,4},{16,8},{20,12},{24,16},{28,20},{1,25},{... | collective-permute-start | bytes 344072 | tf_op jit(solution)/shard_map/ppermute | solution.py:267
  42.8 8.4 %collective-permute-start.7 = (bf16[4,56,256]{2,1,0:T(8,128)(2,1)S(1)}, bf16[4,56,256]{2,1,0:T(8,128)(2,1)S(1)}, u32[]{:S(2)}, u32[]{:S(2)}) collective-permute-start(bf16[4,56,256]{2,1,0:T(8,128)(2,1)S(1)} %slice.14), channel_id=1, source_target_pairs={{0,8},{4,12},{8,16},{12,20},{16,24},{20,28},{24,0},{28,4},{1,9},{5... | collective-permute-start | bytes 344072 | tf_op jit(solution)/shard_map/ppermute | solution.py:267
  43.0 10.4 %collective-permute-start.9 = (bf16[40,56,256]{2,1,0:T(8,128)(2,1)S(1)}, bf16[40,56,256]{2,1,0:T(8,128)(2,1)S(1)}, u32[]{:S(2)}, u32[]{:S(2)}) collective-permute-start(bf16[40,56,256]{2,1,0:T(8,128)(2,1)S(1)} %constant_dynamic-update-slice_fusion.refs_4_), channel_id=1, source_target_pairs={{0,64},{64,0},{1,65},{65,1},{2,66},{66,2},{3,67},{67,3},{4,68},{68... | collective-permute-start | bytes 3440648 | tf_op jit(solution)/shard_map/ppermute | solution.py:267
  51.2 2.2 %collective-permute-start.10 = (bf16[24,56,256]{2,1,0:T(8,128)(2,1)S(1)}, bf16[24,56,256]{2,1,0:T(8,128)(2,1)S(1)}, u32[]{:S(2)}, u32[]{:S(2)}) collective-permute-start(bf16[24,56,256]{2,1,0:T(8,128)(2,1)S(1)} %constant_dynamic-update-slice_fusion.5.refs_5_), channel_id=1, source_target_pairs={{0,64},{64,0},{1,65},{65,1},{2,66},{66,2},{3,67},{67,3},{4,68},{68... | collective-permute-start | bytes 2064392 | tf_op jit(solution)/shard_map/ppermute | solution.py:267

commit v3 on v2

--- a/solution.py
+++ b/solution.py
@@ -121,7 +121,7 @@
                 new.append(peak)
             return tuple(new)
 
-        peaks = lax.fori_loop(0, batches, score, tuple(peaks))
+        peaks = lax.fori_loop(1, batches, score, score(0, tuple(peaks)))
         peaks = [jnp.max(peak, axis=0, keepdims=True) for peak in peaks]
 
         state = []
@@ -144,11 +144,11 @@
                 new.append((total, mixed + mixed_by(values, jnp.concatenate(parts, axis=0))))
             return tuple(new)
 
-        state = lax.fori_loop(0, batches, mix, tuple(state))
+        state = lax.fori_loop(1, batches, mix, mix(0, tuple(state)))
         for u, s in enumerate(spans):
             total, mixed = state[u]
             total = jnp.sum(total, axis=0, keepdims=True)
-            out_ref[s, :ROWS, :] = (mixed / total).astype(jnp.bfloat16).T
+            out_ref[s, :ROWS, :] = (mixed * (1.0 / total)).astype(jnp.bfloat16).T
             level = peaks[u] + jnp.log2(total)
             first = level.astype(jnp.bfloat16).astype(jnp.float32)
             second = (level - first).astype(jnp.bfloat16).astype(jnp.float32)
@@ -188,26 +188,30 @@
 def combine_kernel(parts_ref, out_ref, *, pieces):
     heads = parts_ref.shape[0] // pieces
     three = (lax.broadcasted_iota(jnp.int32, (8, HEAD), 0) < 3).astype(jnp.bfloat16)
-
-    def spread(rows):
+    rest = jnp.zeros((5, HEAD), jnp.float32)
+
+    def spread(row):
+        first = row.astype(jnp.bfloat16).astype(jnp.float32)
+        second = (row - first).astype(jnp.bfloat16).astype(jnp.float32)
+        rows = jnp.concatenate([first, second, row - first - second, rest], axis=0).astype(jnp.bfloat16)
         return lax.dot_general(rows, three, (((0,), (0,)), ((), ())), preferred_element_type=jnp.float32)
 
     for h in range(heads):
-        levels = []
+        shares = [[] for _ in range(pieces)]
+        tails = [parts_ref[h * pieces + y, ROWS:, :].astype(jnp.float32) for y in range(pieces)]
+        for k in range(0, 16, 8):
+            levels = [tail[k : k + 1] + tail[k + 1 : k + 2] + tail[k + 2 : k + 3] for tail in tails]
+            peak = levels[0]
+            for level in levels[1:]:
+                peak = jnp.maximum(peak, level)
+            weights = [jnp.exp2(level - peak) for level in levels]
+            scale = 1.0 / sum(weights)
+            for y in range(pieces):
+                shares[y].append(spread(weights[y] * scale))
+        mixed = jnp.zeros((ROWS, HEAD), jnp.float32)
         for y in range(pieces):
-            tail = parts_ref[h * pieces + y, ROWS:, :].astype(jnp.float32)
-            both = [spread(tail[k * 8 : k * 8 + 8].astype(jnp.bfloat16)) for k in range(2)]
-            levels.append(jnp.concatenate(both, axis=0)[:ROWS])
-        peak = levels[0]
-        for level in levels[1:]:
-            peak = jnp.maximum(peak, level)
-        total = jnp.zeros_like(peak)
-        mixed = jnp.zeros_like(peak)
-        for y in range(pieces):
-            weight = jnp.exp2(levels[y] - peak)
-            total = total + weight
-            mixed = mixed + weight * parts_ref[h * pieces + y, :ROWS, :].astype(jnp.float32)
-        mixed = (mixed / total)
+            share = jnp.concatenate(shares[y], axis=0)[:ROWS]
+            mixed = mixed + share * parts_ref[h * pieces + y, :ROWS, :].astype(jnp.float32)
         for g in range(GROUP):
             at = (h * GROUP + g) * HEAD
             out_ref[:, at : at + HEAD] = mixed[g * SPAN : (g + 1) * SPAN].astype(jnp.bfloat16)

time: 90.4 us -> 88.1 us (0.975)
  blocking collectives: 23.7 us -> 21.6 us
    all_to_all x1, blocking collectives: 23.7 us -> 21.6 us  [per_device(): lax.all_to_all(parts, HEADS + ('yhi',), split_axis=0, concat_axis=0, tile...]
  transfers between devices with their start and end apart: 12 -> 12, of which waited for: 8 -> 8; matrix products, arithmetic and copies ran while one was open for 4% -> 5% of each run, Pallas kernels for 0% -> 0%
where the time goes in v3:
time: 88.1 us; the launch traced here: 87.9 us
  waiting for transfers between devices  26.6 us (30%)
  blocking collectives  21.6 us (25%)
  starting transfers between devices  20.3 us (23%)
  Pallas kernels  15 us (17%)
  local copies, waits for them, and re-layouts  2.26 us (3%)
  other arithmetic  1.09 us (1%)
    all_to_all x1, blocking collectives, per_device(): lax.all_to_all(parts, HEADS + ('yhi',), split_axis=0, concat_axis=0, tile...  21.6 us
    ppermute x11, waiting for transfers between devices, shift(): return lax.ppermute(x, axis, [(i, (i + by) % n) for i in range(n)])  19.5 us
    ppermute x11, starting transfers between devices, shift(): return lax.ppermute(x, axis, [(i, (i + by) % n) for i in range(n)])  14.8 us
    pallas_call x1, Pallas kernels, attend(): pl.pallas_call(kernel, out_shape=jax.ShapeDtypeStruct((query_spans, ROWS...  11.6 us
    all_to_all x1, waiting for transfers between devices, per_device(): lax.all_to_all(packed, HEADS, split_axis=0, concat_axis=0, tiled=True)  7.17 us
    all_to_all x1, starting transfers between devices, per_device(): lax.all_to_all(packed, HEADS, split_axis=0, concat_axis=0, tiled=True)  5.46 us
    pallas_call x1, Pallas kernels, pack(): pl.pallas_call(pack_kernel, out_shape=jax.ShapeDtypeStruct((heads, SPAN,...  2.1 us
  transfers between devices with their start and end apart: 12, of which 8 were waited for; matrix products, arithmetic and copies ran while one was open for 5% of the time, Pallas kernels for 0%

profile of v3, /device:TPU:32, one launch (start us, length us, event | category | flops | bytes accessed | tf_op | source)
XLA Modules:
  0.0 87.9 jit_solution(2680924981098867031)
XLA Ops:
  0.0 2.1 %shard_map.73 = bf16[8,56,768]{2,1,0:T(8,128)(2,1)} custom-call(bf16[56,4096]{1,0:T(8,128)(2,1)} %queries_ref.1, bf16[56,1024]{1,0:T(8,128)(2,1)} %keys_ref.1, bf16[56,1024]{1,0:T(8,128)(2,1)} %values_ref.1), custom_call_target="tpu_custom_call" | custom-call | tf_op jit(solution)/shard_map/pallas_call | solution.py:310
  2.1 5.5 %all-to-all-start = ((bf16[8,56,768]{2,1,0:T(8,128)(2,1)}), bf16[8,56,768]{2,1,0:T(8,128)(2,1)S(1)}, u32[]{:S(2)}, u32[]{:S(2)}) async-start(bf16[8,56,768]{2,1,0:T(8,128)(2,1)} %shard_map.73), calls=%async_computation | async-start | bytes 1376256 | tf_op jit(solution)/shard_map/all_to_all | solution.py:325
  7.7 0.2 reshape.123
  7.9 0.1 copy.26
  8.2 0.6 gather_fusion
  8.9 0.1 copy.27
  9.0 0.6 gather_fusion.1
  9.7 0.1 select_n.117
  9.9 0.4 convert_reduce_fusion
  10.3 0.2 fusion
  10.5 0.2 fusion.1
  10.7 0.2 convert_reduce_fusion.1
  10.9 0.1 select_reduce_fusion.2
  11.1 0.4 select_reduce_fusion
  11.7 7.2 %all-to-all-done = bf16[8,56,768]{2,1,0:T(8,128)(2,1)S(1)} async-done(((bf16[8,56,768]{2,1,0:T(8,128)(2,1)}), bf16[8,56,768]{2,1,0:T(8,128)(2,1)S(1)}, u32[]{:S(2)}, u32[]{:S(2)}) %all-to-all-start) | async-done | bytes 688160 | tf_op jit(solution)/shard_map/all_to_all | solution.py:325
  18.9 0.2 collective-permute-start.2
  19.1 1.9 %collective-permute-start = (bf16[8,56,256]{2,1,0:T(8,128)(2,1)S(1)}, bf16[8,56,256]{2,1,0:T(8,128)(2,1)S(1)}, u32[]{:S(2)}, u32[]{:S(2)}) collective-permute-start(bf16[8,56,256]{2,1,0:T(8,128)(2,1)S(1)} %slice.21), channel_id=1, source_target_pairs={{0,4},{4,8},{8,12},{12,16},{16,20},{20,24},{24,28},{28,0},{1,5},{5... | collective-permute-start | bytes 688136 | tf_op jit(solution)/shard_map/ppermute | solution.py:271
  21.0 2.9 %collective-permute-start.4 = (bf16[8,56,512]{2,1,0:T(8,128)(2,1)S(1)}, bf16[8,56,512]{2,1,0:T(8,128)(2,1)S(1)}, u32[]{:S(2)}, u32[]{:S(2)}) collective-permute-start(bf16[8,56,512]{2,1,0:T(8,128)(2,1)S(1)} %slice.20.refs_2_), channel_id=1, source_target_pairs={{0,2},{2,0},{1,3},{3,1},{4,6},{6,4},{5,7},{7,5},{8,10},{10,8},{9,1... | collective-permute-start | bytes 1376264 | tf_op jit(solution)/shard_map/ppermute | solution.py:271
  23.9 1.7 %collective-permute-done.2 = bf16[8,56,256]{2,1,0:T(8,128)(2,1)S(1)} collective-permute-done((bf16[8,56,256]{2,1,0:T(8,128)(2,1)S(1)}, bf16[8,56,256]{2,1,0:T(8,128)(2,1)S(1)}, u32[]{:S(2)}, u32[]{:S(2)}) %collective-permute-start.2) | collective-permute-done | bytes 229408 | tf_op jit(solution)/shard_map/ppermute | solution.py:271
  25.6 3.3 %collective-permute-start.3 = (bf16[8,56,256]{2,1,0:T(8,128)(2,1)S(1)}, bf16[8,56,256]{2,1,0:T(8,128)(2,1)S(1)}, u32[]{:S(2)}, u32[]{:S(2)}) collective-permute-start(bf16[8,56,256]{2,1,0:T(8,128)(2,1)S(1)} %collective-permute-done.2), channel_id=1, source_target_pairs={{0,28},{4,0},{8,4},{12,8},{16,12},{20,16},{24,20},{28,24},{1,29},{... | collective-permute-start | bytes 688136 | tf_op jit(solution)/shard_map/ppermute | solution.py:271
  28.9 0.5 collective-permute-done
  29.4 4.2 %collective-permute-done.4.refs_3_ = bf16[8,56,512]{2,1,0:T(8,128)(2,1)S(1)} collective-permute-done((bf16[8,56,512]{2,1,0:T(8,128)(2,1)S(1)}, bf16[8,56,512]{2,1,0:T(8,128)(2,1)S(1)}, u32[]{:S(2)}, u32[]{:S(2)}) %collective-permute-start.4) | collective-permute-done | bytes 458784 | tf_op jit(solution)/shard_map/ppermute | solution.py:271
  33.6 3.0 %collective-permute-done.1 = bf16[8,56,256]{2,1,0:T(8,128)(2,1)S(1)} collective-permute-done((bf16[8,56,256]{2,1,0:T(8,128)(2,1)S(1)}, bf16[8,56,256]{2,1,0:T(8,128)(2,1)S(1)}, u32[]{:S(2)}, u32[]{:S(2)}) %collective-permute-start.1) | collective-permute-done | bytes 229408 | tf_op jit(solution)/shard_map/ppermute | solution.py:271
  36.7 3.3 %collective-permute-start.6 = (bf16[8,56,256]{2,1,0:T(8,128)(2,1)S(1)}, bf16[8,56,256]{2,1,0:T(8,128)(2,1)S(1)}, u32[]{:S(2)}, u32[]{:S(2)}) collective-permute-start(bf16[8,56,256]{2,1,0:T(8,128)(2,1)S(1)} %collective-permute-done.3), channel_id=1, source_target_pairs={{0,28},{4,0},{8,4},{12,8},{16,12},{20,16},{24,20},{28,24},{1,29},{... | collective-permute-start | bytes 688136 | tf_op jit(solution)/shard_map/ppermute | solution.py:271
  40.0 2.7 %collective-permute-start.8 = (bf16[4,56,256]{2,1,0:T(8,128)(2,1)S(1)}, bf16[4,56,256]{2,1,0:T(8,128)(2,1)S(1)}, u32[]{:S(2)}, u32[]{:S(2)}) collective-permute-start(bf16[4,56,256]{2,1,0:T(8,128)(2,1)S(1)} %slice.15), channel_id=1, source_target_pairs={{0,24},{4,28},{8,0},{12,4},{16,8},{20,12},{24,16},{28,20},{1,25},{... | collective-permute-start | bytes 344072 | tf_op jit(solution)/shard_map/ppermute | solution.py:271
  42.8 0.2 collective-permute-start.7
  43.1 2.6 %collective-permute-done.5 = bf16[8,56,256]{2,1,0:T(8,128)(2,1)S(1)} collective-permute-done((bf16[8,56,256]{2,1,0:T(8,128)(2,1)S(1)}, bf16[8,56,256]{2,1,0:T(8,128)(2,1)S(1)}, u32[]{:S(2)}, u32[]{:S(2)}) %collective-permute-start.5) | collective-permute-done | bytes 229408 | tf_op jit(solution)/shard_map/ppermute | solution.py:271
  45.8 5.3 %collective-permute-done.7 = bf16[4,56,256]{2,1,0:T(8,128)(2,1)S(1)} collective-permute-done((bf16[4,56,256]{2,1,0:T(8,128)(2,1)S(1)}, bf16[4,56,256]{2,1,0:T(8,128)(2,1)S(1)}, u32[]{:S(2)}, u32[]{:S(2)}) %collective-permute-start.7) | collective-permute-done | bytes 114720 | tf_op jit(solution)/shard_map/ppermute | solution.py:271
  51.3 2.1 %collective-permute-done.10.refs_7_ = bf16[24,56,256]{2,1,0:T(8,128)(2,1)S(1)} collective-permute-done((bf16[24,56,256]{2,1,0:T(8,128)(2,1)S(1)}, bf16[24,56,256]{2,1,0:T(8,128)(2,1)S(1)}, u32[]{:S(2)}, u32[]{:S(2)}) %collective-permute-start.10) | collective-permute-done | bytes 688160 | tf_op jit(solution)/shard_map/ppermute | solution.py:271
  53.4 11.6 %shard_map.74 = bf16[16,240,128]{2,1,0:T(8,128)(2,1)S(1)} custom-call(s32[16,256]{1,0:T(8,128)S(1)} %pad_add_fusion.refs_0_, bf16[128,128]{1,0:T(8,128)(2,1)S(1)} %concatenate.13.refs_1_, bf16[8,56,512]{2,1,0:T(8,128)(2,1)S(1)} %slice.20.refs_2_, bf16[8,56,512]{2,1,0:T(8,128)(2,1)S(1)} %collective-permute-done.4.refs_3_, ...), custom_call_target="tpu_custom_call" | custom-call | tf_op jit(solution)/shard_map/pallas_call | solution.py:172
  65.1 21.6 %all_to_all.10.parts_ref = bf16[16,240,128]{2,1,0:T(8,128)(2,1)S(1)} all-to-all(bf16[16,240,128]{2,1,0:T(8,128)(2,1)S(1)} %shard_map.74), channel_id=1, replica_groups=mesh['xhi'=2,'core'=2,'xlo'=2,'z'=8,'yhi'=2,'ylo'=2] {'xhi','xlo','ylo',..., dimensions={0} | all-to-all | bytes 1966080 | tf_op jit(solution)/shard_map/all_to_all | solution.py:342
  86.7 1.3 %shard_map.75 = bf16[56,4096]{1,0:T(8,128)(2,1)} custom-call(bf16[16,240,128]{2,1,0:T(8,128)(2,1)S(1)} %all_to_all.10.parts_ref), custom_call_target="tpu_custom_call" | custom-call | tf_op jit(solution)/shard_map/pallas_call | solution.py:227
  (51 shorter events, 1.2 us)
Async XLA Ops:
  0.0 7.7 %copy-start.1 = (s32[8]{0:T(128)S(1)}, s32[8]{0:T(128)}, u32[]{:S(2)}) copy-start(s32[8]{0:T(128)} %constant.132.clone) | copy-start | bytes 100
  0.0 7.7 %copy-start = (s32[256]{0:T(256)S(1)}, s32[256]{0:T(256)}, u32[]{:S(2)}) copy-start(s32[256]{0:T(256)} %param.10) | copy-start | bytes 3076
  2.1 7.8 %copy-start.2 = (s32[256,256]{1,0:T(8,128)S(1)}, s32[256,256]{1,0:T(8,128)}, u32[]{:S(2)}) copy-start(s32[256,256]{1,0:T(8,128)} %param.11) | copy-start | bytes 786436
  2.1 8.4 %copy-start.3 = (s32[256]{0:T(256)S(1)}, s32[256]{0:T(256)}, u32[]{:S(2)}) copy-start(s32[256]{0:T(256)} %param.12) | copy-start | bytes 3076
  2.1 16.7 %all-to-all-start = ((bf16[8,56,768]{2,1,0:T(8,128)(2,1)}), bf16[8,56,768]{2,1,0:T(8,128)(2,1)S(1)}, u32[]{:S(2)}, u32[]{:S(2)}) async-start(bf16[8,56,768]{2,1,0:T(8,128)(2,1)} %shard_map.73), calls=%async_computation | async-start | bytes 1376256 | tf_op jit(solution)/shard_map/all_to_all | solution.py:325
  18.9 6.7 %collective-permute-start.2 = (bf16[8,56,256]{2,1,0:T(8,128)(2,1)S(1)}, bf16[8,56,256]{2,1,0:T(8,128)(2,1)S(1)}, u32[]{:S(2)}, u32[]{:S(2)}) collective-permute-start(bf16[8,56,256]{2,1,0:T(8,128)(2,1)S(1)} %slice.21), channel_id=1, source_target_pairs={{0,28},{4,0},{8,4},{12,8},{16,12},{20,16},{24,20},{28,24},{1,29},{... | collective-permute-start | bytes 688136 | tf_op jit(solution)/shard_map/ppermute | solution.py:271
  19.1 10.3 %collective-permute-start = (bf16[8,56,256]{2,1,0:T(8,128)(2,1)S(1)}, bf16[8,56,256]{2,1,0:T(8,128)(2,1)S(1)}, u32[]{:S(2)}, u32[]{:S(2)}) collective-permute-start(bf16[8,56,256]{2,1,0:T(8,128)(2,1)S(1)} %slice.21), channel_id=1, source_target_pairs={{0,4},{4,8},{8,12},{12,16},{16,20},{20,24},{24,28},{28,0},{1,5},{5... | collective-permute-start | bytes 688136 | tf_op jit(solution)/shard_map/ppermute | solution.py:271
  21.0 12.6 %collective-permute-start.4 = (bf16[8,56,512]{2,1,0:T(8,128)(2,1)S(1)}, bf16[8,56,512]{2,1,0:T(8,128)(2,1)S(1)}, u32[]{:S(2)}, u32[]{:S(2)}) collective-permute-start(bf16[8,56,512]{2,1,0:T(8,128)(2,1)S(1)} %slice.20.refs_2_), channel_id=1, source_target_pairs={{0,2},{2,0},{1,3},{3,1},{4,6},{6,4},{5,7},{7,5},{8,10},{10,8},{9,1... | collective-permute-start | bytes 1376264 | tf_op jit(solution)/shard_map/ppermute | solution.py:271
  25.6 8.0 %collective-permute-start.3 = (bf16[8,56,256]{2,1,0:T(8,128)(2,1)S(1)}, bf16[8,56,256]{2,1,0:T(8,128)(2,1)S(1)}, u32[]{:S(2)}, u32[]{:S(2)}) collective-permute-start(bf16[8,56,256]{2,1,0:T(8,128)(2,1)S(1)} %collective-permute-done.2), channel_id=1, source_target_pairs={{0,28},{4,0},{8,4},{12,8},{16,12},{20,16},{24,20},{28,24},{1,29},{... | collective-permute-start | bytes 688136 | tf_op jit(solution)/shard_map/ppermute | solution.py:271
  29.4 7.2 %collective-permute-start.1 = (bf16[8,56,256]{2,1,0:T(8,128)(2,1)S(1)}, bf16[8,56,256]{2,1,0:T(8,128)(2,1)S(1)}, u32[]{:S(2)}, u32[]{:S(2)}) collective-permute-start(bf16[8,56,256]{2,1,0:T(8,128)(2,1)S(1)} %collective-permute-done), channel_id=1, source_target_pairs={{0,4},{4,8},{8,12},{12,16},{16,20},{20,24},{24,28},{28,0},{1,5},{5... | collective-permute-start | bytes 688136 | tf_op jit(solution)/shard_map/ppermute | solution.py:271
  36.6 9.1 %collective-permute-start.5 = (bf16[8,56,256]{2,1,0:T(8,128)(2,1)S(1)}, bf16[8,56,256]{2,1,0:T(8,128)(2,1)S(1)}, u32[]{:S(2)}, u32[]{:S(2)}) collective-permute-start(bf16[8,56,256]{2,1,0:T(8,128)(2,1)S(1)} %collective-permute-done.1), channel_id=1, source_target_pairs={{0,4},{4,8},{8,12},{12,16},{16,20},{20,24},{24,28},{28,0},{1,5},{5... | collective-permute-start | bytes 688136 | tf_op jit(solution)/shard_map/ppermute | solution.py:271
  36.7 9.0 %collective-permute-start.6 = (bf16[8,56,256]{2,1,0:T(8,128)(2,1)S(1)}, bf16[8,56,256]{2,1,0:T(8,128)(2,1)S(1)}, u32[]{:S(2)}, u32[]{:S(2)}) collective-permute-start(bf16[8,56,256]{2,1,0:T(8,128)(2,1)S(1)} %collective-permute-done.3), channel_id=1, source_target_pairs={{0,28},{4,0},{8,4},{12,8},{16,12},{20,16},{24,20},{28,24},{1,29},{... | collective-permute-start | bytes 688136 | tf_op jit(solution)/shard_map/ppermute | solution.py:271
  40.0 11.1 %collective-permute-start.8 = (bf16[4,56,256]{2,1,0:T(8,128)(2,1)S(1)}, bf16[4,56,256]{2,1,0:T(8,128)(2,1)S(1)}, u32[]{:S(2)}, u32[]{:S(2)}) collective-permute-start(bf16[4,56,256]{2,1,0:T(8,128)(2,1)S(1)} %slice.15), channel_id=1, source_target_pairs={{0,24},{4,28},{8,0},{12,4},{16,8},{20,12},{24,16},{28,20},{1,25},{... | collective-permute-start | bytes 344072 | tf_op jit(solution)/shard_map/ppermute | solution.py:271
  42.8 8.4 %collective-permute-start.7 = (bf16[4,56,256]{2,1,0:T(8,128)(2,1)S(1)}, bf16[4,56,256]{2,1,0:T(8,128)(2,1)S(1)}, u32[]{:S(2)}, u32[]{:S(2)}) collective-permute-start(bf16[4,56,256]{2,1,0:T(8,128)(2,1)S(1)} %slice.14), channel_id=1, source_target_pairs={{0,8},{4,12},{8,16},{12,20},{16,24},{20,28},{24,0},{28,4},{1,9},{5... | collective-permute-start | bytes 344072 | tf_op jit(solution)/shard_map/ppermute | solution.py:271
  43.0 10.4 %collective-permute-start.9 = (bf16[40,56,256]{2,1,0:T(8,128)(2,1)S(1)}, bf16[40,56,256]{2,1,0:T(8,128)(2,1)S(1)}, u32[]{:S(2)}, u32[]{:S(2)}) collective-permute-start(bf16[40,56,256]{2,1,0:T(8,128)(2,1)S(1)} %constant_dynamic-update-slice_fusion.refs_4_), channel_id=1, source_target_pairs={{0,64},{64,0},{1,65},{65,1},{2,66},{66,2},{3,67},{67,3},{4,68},{68... | collective-permute-start | bytes 3440648 | tf_op jit(solution)/shard_map/ppermute | solution.py:271
  51.2 2.2 %collective-permute-start.10 = (bf16[24,56,256]{2,1,0:T(8,128)(2,1)S(1)}, bf16[24,56,256]{2,1,0:T(8,128)(2,1)S(1)}, u32[]{:S(2)}, u32[]{:S(2)}) collective-permute-start(bf16[24,56,256]{2,1,0:T(8,128)(2,1)S(1)} %constant_dynamic-update-slice_fusion.5.refs_5_), channel_id=1, source_target_pairs={{0,64},{64,0},{1,65},{65,1},{2,66},{66,2},{3,67},{67,3},{4,68},{68... | collective-permute-start | bytes 2064392 | tf_op jit(solution)/shard_map/ppermute | solution.py:271

commit v4 on v3

--- a/solution.py
+++ b/solution.py
@@ -14,7 +14,8 @@
 PADDED = 64
 ROWS = GROUP * SPAN
 EXTRA = 16
-BATCH = 8
+FIRST = 12
+BATCH = 4
 TOGETHER = 4
 NEG = -1e30
 LOG2E = math.log2(math.e)
@@ -52,7 +53,7 @@
     summary = (sums[...] / math.sqrt(SPAN)).astype(jnp.bfloat16)
 
     summary_keys = jnp.concatenate([summary[:, :HEAD], mask_ref[...]], axis=1)
-    none = jnp.zeros((PADDED, HEAD), jnp.bfloat16)
+    none = jnp.zeros(((FIRST + 1) * PADDED, HEAD), jnp.bfloat16)
     span_row = lax.broadcasted_iota(jnp.int32, (HEAD, ROWS), 0)
     gap = jnp.zeros((PADDED - SPAN, HEAD), jnp.bfloat16)
     blank = jnp.zeros((PADDED - SPAN, ROWS), jnp.float32)
@@ -89,7 +90,7 @@
         most = counts[0]
         for c in counts[1:]:
             most = jnp.maximum(most, c)
-        batches = (most + BATCH - 1) // BATCH
+        batches = jnp.maximum(most - FIRST + BATCH - 1, 0) // BATCH
 
         for u, s in enumerate(spans):
             rows = jnp.where(s % 2 == side, ours_ref[s // 2], theirs_ref[s // 2]).astype(jnp.float32)
@@ -97,45 +98,57 @@
             turned[u, :HEAD] = rows.astype(jnp.bfloat16).T
             turned[u, HEAD:] = (span_row == s).astype(jnp.bfloat16)
 
+        starts = [[jnp.maximum(owns[u], 0)] + [table_ref[s, k] for k in range(FIRST)] for u, s in enumerate(spans)]
         peaks = []
         for u, s in enumerate(spans):
-            keys = jnp.concatenate([summary_keys, jnp.concatenate([pile([jnp.maximum(owns[u], 0)], key_lanes), none], axis=1)], axis=0)
+            blocks = pile(starts[u], key_lanes)
+            keys = jnp.concatenate([summary_keys, jnp.concatenate([blocks, none], axis=1)], axis=0)
             scores = jnp.dot(keys, turned[u], preferred_element_type=jnp.float32) * SCORE_SCALE
             far = scores[:key_spans] + SUMMARY_BIAS
-            near = scores[key_spans : key_spans + SPAN] + (causal + jnp.where(owns[u] >= 0, 0.0, NEG))
             base[u, :key_spans] = far
-            base[u, key_spans:] = near
-            peaks.append(jnp.maximum(high(far), high(near)))
+            peak = high(far)
+            for k in range(FIRST + 1):
+                at = key_spans + k * PADDED
+                if k == 0:
+                    part = scores[at : at + SPAN] + (causal + jnp.where(owns[u] >= 0, 0.0, NEG))
+                else:
+                    part = scores[at : at + SPAN] + jnp.where(k - 1 < counts[u], 0.0, NEG)
+                base[u, key_spans + k * SPAN : key_spans + (k + 1) * SPAN] = part
+                peak = jnp.maximum(peak, high(part))
+            peaks.append(peak)
 
         def score(t, peaks):
             new = []
             for u, s in enumerate(spans):
-                keys = pile([table_ref[s, t * BATCH + k] for k in range(BATCH)], key_lanes)
+                keys = pile([table_ref[s, FIRST + t * BATCH + k] for k in range(BATCH)], key_lanes)
                 scores = jnp.dot(keys, turned[u, :HEAD], preferred_element_type=jnp.float32) * SCORE_SCALE
                 peak = peaks[u]
                 for k in range(BATCH):
                     part = scores[k * PADDED : k * PADDED + SPAN]
-                    part = part + jnp.where(t * BATCH + k < counts[u], 0.0, NEG)
+                    part = part + jnp.where(FIRST + t * BATCH + k < counts[u], 0.0, NEG)
                     held[u, t, k * SPAN : (k + 1) * SPAN] = part
                     peak = jnp.maximum(peak, high(part))
                 new.append(peak)
             return tuple(new)
 
-        peaks = lax.fori_loop(1, batches, score, score(0, tuple(peaks)))
+        peaks = lax.fori_loop(0, batches, score, tuple(peaks))
         peaks = [jnp.max(peak, axis=0, keepdims=True) for peak in peaks]
 
         state = []
         for u, s in enumerate(spans):
             weight = jnp.exp2(base[u] - peaks[u])
-            values = jnp.concatenate([summary[:, HEAD:], pile([jnp.maximum(owns[u], 0)], value_lanes)], axis=0)
-            total = add(weight)
-            state.append((total, mixed_by(values, jnp.concatenate([weight, blank], axis=0))))
+            values = jnp.concatenate([summary[:, HEAD:], pile(starts[u], value_lanes)], axis=0)
+            parts = [weight[:key_spans]]
+            for k in range(FIRST + 1):
+                at = key_spans + k * SPAN
+                parts += [weight[at : at + SPAN], blank]
+            state.append((add(weight), mixed_by(values, jnp.concatenate(parts, axis=0))))
 
         def mix(t, state):
             new = []
             for u, s in enumerate(spans):
                 total, mixed = state[u]
-                values = pile([table_ref[s, t * BATCH + k] for k in range(BATCH)], value_lanes)
+                values = pile([table_ref[s, FIRST + t * BATCH + k] for k in range(BATCH)], value_lanes)
                 weight = jnp.exp2(held[u, t] - peaks[u])
                 total = total + add(weight)
                 parts = []
@@ -144,7 +157,7 @@
                 new.append((total, mixed + mixed_by(values, jnp.concatenate(parts, axis=0))))
             return tuple(new)
 
-        state = lax.fori_loop(1, batches, mix, mix(0, tuple(state)))
+        state = lax.fori_loop(0, batches, mix, tuple(state))
         for u, s in enumerate(spans):
             total, mixed = state[u]
             total = jnp.sum(total, axis=0, keepdims=True)
@@ -177,7 +190,7 @@
         scratch_shapes=[
             pltpu.VMEM((key_spans, SPAN, 2 * HEAD), jnp.bfloat16),
             pltpu.VMEM((key_spans, 2 * HEAD), jnp.float32),
-            pltpu.VMEM((TOGETHER, key_spans + SPAN, ROWS), jnp.float32),
+            pltpu.VMEM((TOGETHER, key_spans + (FIRST + 1) * SPAN, ROWS), jnp.float32),
             pltpu.VMEM((TOGETHER, key_spans // BATCH, BATCH * SPAN, ROWS), jnp.float32),
             pltpu.VMEM((TOGETHER, 2 * HEAD, ROWS), jnp.bfloat16),
         ],

time: 88.1 us -> 87.5 us (level)
  the two profiles are of different devices: /device:TPU:32 before, /device:TPU:1 now
where the time goes in v4:
time: 87.5 us; the launch traced here: 86.8 us
  starting transfers between devices  32 us (37%)
  blocking collectives  20.6 us (24%)
  waiting for transfers between devices  15.6 us (18%)
  Pallas kernels  14.3 us (16%)
  local copies, waits for them, and re-layouts  2.27 us (3%)
  other arithmetic  1.09 us (1%)
    ppermute x11, starting transfers between devices, shift(): return lax.ppermute(x, axis, [(i, (i + by) % n) for i in range(n)])  26 us
    all_to_all x1, blocking collectives, per_device(): lax.all_to_all(parts, HEADS + ('yhi',), split_axis=0, concat_axis=0, tile...  20.6 us
    pallas_call x1, Pallas kernels, attend(): pl.pallas_call(kernel, out_shape=jax.ShapeDtypeStruct((query_spans, ROWS...  10.9 us
    ppermute x11, waiting for transfers between devices, shift(): return lax.ppermute(x, axis, [(i, (i + by) % n) for i in range(n)])  9.01 us
    all_to_all x1, waiting for transfers between devices, per_device(): lax.all_to_all(packed, HEADS, split_axis=0, concat_axis=0, tiled=True)  6.57 us
    all_to_all x1, starting transfers between devices, per_device(): lax.all_to_all(packed, HEADS, split_axis=0, concat_axis=0, tiled=True)  6.01 us
    pallas_call x1, Pallas kernels, pack(): pl.pallas_call(pack_kernel, out_shape=jax.ShapeDtypeStruct((heads, SPAN,...  2.1 us
  transfers between devices with their start and end apart: 12, of which 6 were waited for; matrix products, arithmetic and copies ran while one was open for 5% of the time, Pallas kernels for 0%

profile of v4, /device:TPU:1, one launch (start us, length us, event | category | flops | bytes accessed | tf_op | source)
XLA Modules:
  0.0 86.8 jit_solution(14994040649385894642)
XLA Ops:
  0.0 2.1 %shard_map.73 = bf16[8,56,768]{2,1,0:T(8,128)(2,1)} custom-call(bf16[56,4096]{1,0:T(8,128)(2,1)} %queries_ref.1, bf16[56,1024]{1,0:T(8,128)(2,1)} %keys_ref.1, bf16[56,1024]{1,0:T(8,128)(2,1)} %values_ref.1), custom_call_target="tpu_custom_call" | custom-call | tf_op jit(solution)/shard_map/pallas_call | solution.py:323
  2.1 6.0 %all-to-all-start = ((bf16[8,56,768]{2,1,0:T(8,128)(2,1)}), bf16[8,56,768]{2,1,0:T(8,128)(2,1)S(1)}, u32[]{:S(2)}, u32[]{:S(2)}) async-start(bf16[8,56,768]{2,1,0:T(8,128)(2,1)} %shard_map.73), calls=%async_computation | async-start | bytes 1376256 | tf_op jit(solution)/shard_map/all_to_all | solution.py:338
  8.2 0.2 reshape.123
  8.5 0.1 copy.26
  8.6 0.1 copy.29
  8.8 0.6 gather_fusion
  9.4 0.1 copy.27
  9.6 0.6 gather_fusion.1
  10.3 0.1 select_n.117
  10.4 0.4 convert_reduce_fusion
  10.8 0.2 fusion
  11.1 0.2 fusion.1
  11.3 0.2 convert_reduce_fusion.1
  11.5 0.1 select_reduce_fusion.2
  11.6 0.4 select_reduce_fusion
  12.0 0.1 select_convert_fusion
  12.2 6.6 %all-to-all-done = bf16[8,56,768]{2,1,0:T(8,128)(2,1)S(1)} async-done(((bf16[8,56,768]{2,1,0:T(8,128)(2,1)}), bf16[8,56,768]{2,1,0:T(8,128)(2,1)S(1)}, u32[]{:S(2)}, u32[]{:S(2)}) %all-to-all-start) | async-done | bytes 688160 | tf_op jit(solution)/shard_map/all_to_all | solution.py:338
  18.8 5.7 %collective-permute-start.2 = (bf16[8,56,256]{2,1,0:T(8,128)(2,1)S(1)}, bf16[8,56,256]{2,1,0:T(8,128)(2,1)S(1)}, u32[]{:S(2)}, u32[]{:S(2)}) collective-permute-start(bf16[8,56,256]{2,1,0:T(8,128)(2,1)S(1)} %slice.21), channel_id=1, source_target_pairs={{0,28},{4,0},{8,4},{12,8},{16,12},{20,16},{24,20},{28,24},{1,29},{... | collective-permute-start | bytes 688136 | tf_op jit(solution)/shard_map/ppermute | solution.py:284
  24.5 2.6 %collective-permute-start.4 = (bf16[8,56,512]{2,1,0:T(8,128)(2,1)S(1)}, bf16[8,56,512]{2,1,0:T(8,128)(2,1)S(1)}, u32[]{:S(2)}, u32[]{:S(2)}) collective-permute-start(bf16[8,56,512]{2,1,0:T(8,128)(2,1)S(1)} %slice.20.refs_2_), channel_id=1, source_target_pairs={{0,2},{2,0},{1,3},{3,1},{4,6},{6,4},{5,7},{7,5},{8,10},{10,8},{9,1... | collective-permute-start | bytes 1376264 | tf_op jit(solution)/shard_map/ppermute | solution.py:284
  27.1 0.7 collective-permute-done.2
  27.8 3.4 %collective-permute-start.3 = (bf16[8,56,256]{2,1,0:T(8,128)(2,1)S(1)}, bf16[8,56,256]{2,1,0:T(8,128)(2,1)S(1)}, u32[]{:S(2)}, u32[]{:S(2)}) collective-permute-start(bf16[8,56,256]{2,1,0:T(8,128)(2,1)S(1)} %collective-permute-done.2), channel_id=1, source_target_pairs={{0,28},{4,0},{8,4},{12,8},{16,12},{20,16},{24,20},{28,24},{1,29},{... | collective-permute-start | bytes 688136 | tf_op jit(solution)/shard_map/ppermute | solution.py:284
  31.3 4.9 %collective-permute-done.4.refs_3_ = bf16[8,56,512]{2,1,0:T(8,128)(2,1)S(1)} collective-permute-done((bf16[8,56,512]{2,1,0:T(8,128)(2,1)S(1)}, bf16[8,56,512]{2,1,0:T(8,128)(2,1)S(1)}, u32[]{:S(2)}, u32[]{:S(2)}) %collective-permute-start.4) | collective-permute-done | bytes 458784 | tf_op jit(solution)/shard_map/ppermute | solution.py:284
  36.2 1.4 %collective-permute-done.1 = bf16[8,56,256]{2,1,0:T(8,128)(2,1)S(1)} collective-permute-done((bf16[8,56,256]{2,1,0:T(8,128)(2,1)S(1)}, bf16[8,56,256]{2,1,0:T(8,128)(2,1)S(1)}, u32[]{:S(2)}, u32[]{:S(2)}) %collective-permute-start.1) | collective-permute-done | bytes 229408 | tf_op jit(solution)/shard_map/ppermute | solution.py:284
  37.7 2.7 %collective-permute-start.6 = (bf16[8,56,256]{2,1,0:T(8,128)(2,1)S(1)}, bf16[8,56,256]{2,1,0:T(8,128)(2,1)S(1)}, u32[]{:S(2)}, u32[]{:S(2)}) collective-permute-start(bf16[8,56,256]{2,1,0:T(8,128)(2,1)S(1)} %collective-permute-done.3), channel_id=1, source_target_pairs={{0,28},{4,0},{8,4},{12,8},{16,12},{20,16},{24,20},{28,24},{1,29},{... | collective-permute-start | bytes 688136 | tf_op jit(solution)/shard_map/ppermute | solution.py:284
  40.5 2.4 %collective-permute-start.7 = (bf16[4,56,256]{2,1,0:T(8,128)(2,1)S(1)}, bf16[4,56,256]{2,1,0:T(8,128)(2,1)S(1)}, u32[]{:S(2)}, u32[]{:S(2)}) collective-permute-start(bf16[4,56,256]{2,1,0:T(8,128)(2,1)S(1)} %slice.14), channel_id=1, source_target_pairs={{0,8},{4,12},{8,16},{12,20},{16,24},{20,28},{24,0},{28,4},{1,9},{5... | collective-permute-start | bytes 344072 | tf_op jit(solution)/shard_map/ppermute | solution.py:284
  42.9 4.8 %collective-permute-start.9 = (bf16[40,56,256]{2,1,0:T(8,128)(2,1)S(1)}, bf16[40,56,256]{2,1,0:T(8,128)(2,1)S(1)}, u32[]{:S(2)}, u32[]{:S(2)}) collective-permute-start(bf16[40,56,256]{2,1,0:T(8,128)(2,1)S(1)} %constant_dynamic-update-slice_fusion.refs_4_), channel_id=1, source_target_pairs={{0,64},{64,0},{1,65},{65,1},{2,66},{66,2},{3,67},{67,3},{4,68},{68... | collective-permute-start | bytes 3440648 | tf_op jit(solution)/shard_map/ppermute | solution.py:284
  47.8 0.2 collective-permute-done.7
  48.0 4.3 %collective-permute-start.10 = (bf16[24,56,256]{2,1,0:T(8,128)(2,1)S(1)}, bf16[24,56,256]{2,1,0:T(8,128)(2,1)S(1)}, u32[]{:S(2)}, u32[]{:S(2)}) collective-permute-start(bf16[24,56,256]{2,1,0:T(8,128)(2,1)S(1)} %constant_dynamic-update-slice_fusion.5.refs_5_), channel_id=1, source_target_pairs={{0,64},{64,0},{1,65},{65,1},{2,66},{66,2},{3,67},{67,3},{4,68},{68... | collective-permute-start | bytes 2064392 | tf_op jit(solution)/shard_map/ppermute | solution.py:284
  52.3 1.8 %collective-permute-done.10.refs_7_ = bf16[24,56,256]{2,1,0:T(8,128)(2,1)S(1)} collective-permute-done((bf16[24,56,256]{2,1,0:T(8,128)(2,1)S(1)}, bf16[24,56,256]{2,1,0:T(8,128)(2,1)S(1)}, u32[]{:S(2)}, u32[]{:S(2)}) %collective-permute-start.10) | collective-permute-done | bytes 688160 | tf_op jit(solution)/shard_map/ppermute | solution.py:284
  54.0 10.9 %shard_map.74 = bf16[16,240,128]{2,1,0:T(8,128)(2,1)S(1)} custom-call(s32[16,256]{1,0:T(8,128)S(1)} %pad_add_fusion.refs_0_, bf16[128,128]{1,0:T(8,128)(2,1)S(1)} %concatenate.13.refs_1_, bf16[8,56,512]{2,1,0:T(8,128)(2,1)S(1)} %slice.20.refs_2_, bf16[8,56,512]{2,1,0:T(8,128)(2,1)S(1)} %collective-permute-done.4.refs_3_, ...), custom_call_target="tpu_custom_call" | custom-call | tf_op jit(solution)/shard_map/pallas_call | solution.py:185
  64.9 20.6 %all_to_all.10.parts_ref = bf16[16,240,128]{2,1,0:T(8,128)(2,1)S(1)} all-to-all(bf16[16,240,128]{2,1,0:T(8,128)(2,1)S(1)} %shard_map.74), channel_id=1, replica_groups=mesh['xhi'=2,'core'=2,'xlo'=2,'z'=8,'yhi'=2,'ylo'=2] {'xhi','xlo','ylo',..., dimensions={0} | all-to-all | bytes 1966080 | tf_op jit(solution)/shard_map/all_to_all | solution.py:355
  85.5 1.3 %shard_map.75 = bf16[56,4096]{1,0:T(8,128)(2,1)} custom-call(bf16[16,240,128]{2,1,0:T(8,128)(2,1)S(1)} %all_to_all.10.parts_ref), custom_call_target="tpu_custom_call" | custom-call | tf_op jit(solution)/shard_map/pallas_call | solution.py:240
  (51 shorter events, 0.9 us)
Async XLA Ops:
  0.0 8.2 %copy-start.1 = (s32[8]{0:T(128)S(1)}, s32[8]{0:T(128)}, u32[]{:S(2)}) copy-start(s32[8]{0:T(128)} %constant.132.clone) | copy-start | bytes 100
  0.0 8.2 %copy-start = (s32[256]{0:T(256)S(1)}, s32[256]{0:T(256)}, u32[]{:S(2)}) copy-start(s32[256]{0:T(256)} %param.10) | copy-start | bytes 3076
  2.1 8.3 %copy-start.2 = (s32[256,256]{1,0:T(8,128)S(1)}, s32[256,256]{1,0:T(8,128)}, u32[]{:S(2)}) copy-start(s32[256,256]{1,0:T(8,128)} %param.11) | copy-start | bytes 786436
  2.1 8.9 %copy-start.3 = (s32[256]{0:T(256)S(1)}, s32[256]{0:T(256)}, u32[]{:S(2)}) copy-start(s32[256]{0:T(256)} %param.12) | copy-start | bytes 3076
  2.1 16.6 %all-to-all-start = ((bf16[8,56,768]{2,1,0:T(8,128)(2,1)}), bf16[8,56,768]{2,1,0:T(8,128)(2,1)S(1)}, u32[]{:S(2)}, u32[]{:S(2)}) async-start(bf16[8,56,768]{2,1,0:T(8,128)(2,1)} %shard_map.73), calls=%async_computation | async-start | bytes 1376256 | tf_op jit(solution)/shard_map/all_to_all | solution.py:338
  18.8 9.0 %collective-permute-start.2 = (bf16[8,56,256]{2,1,0:T(8,128)(2,1)S(1)}, bf16[8,56,256]{2,1,0:T(8,128)(2,1)S(1)}, u32[]{:S(2)}, u32[]{:S(2)}) collective-permute-start(bf16[8,56,256]{2,1,0:T(8,128)(2,1)S(1)} %slice.21), channel_id=1, source_target_pairs={{0,28},{4,0},{8,4},{12,8},{16,12},{20,16},{24,20},{28,24},{1,29},{... | collective-permute-start | bytes 688136 | tf_op jit(solution)/shard_map/ppermute | solution.py:284
  24.5 6.7 %collective-permute-start = (bf16[8,56,256]{2,1,0:T(8,128)(2,1)S(1)}, bf16[8,56,256]{2,1,0:T(8,128)(2,1)S(1)}, u32[]{:S(2)}, u32[]{:S(2)}) collective-permute-start(bf16[8,56,256]{2,1,0:T(8,128)(2,1)S(1)} %slice.21), channel_id=1, source_target_pairs={{0,4},{4,8},{8,12},{12,16},{16,20},{20,24},{24,28},{28,0},{1,5},{5... | collective-permute-start | bytes 688136 | tf_op jit(solution)/shard_map/ppermute | solution.py:284
  24.5 11.7 %collective-permute-start.4 = (bf16[8,56,512]{2,1,0:T(8,128)(2,1)S(1)}, bf16[8,56,512]{2,1,0:T(8,128)(2,1)S(1)}, u32[]{:S(2)}, u32[]{:S(2)}) collective-permute-start(bf16[8,56,512]{2,1,0:T(8,128)(2,1)S(1)} %slice.20.refs_2_), channel_id=1, source_target_pairs={{0,2},{2,0},{1,3},{3,1},{4,6},{6,4},{5,7},{7,5},{8,10},{10,8},{9,1... | collective-permute-start | bytes 1376264 | tf_op jit(solution)/shard_map/ppermute | solution.py:284
  27.8 8.3 %collective-permute-start.3 = (bf16[8,56,256]{2,1,0:T(8,128)(2,1)S(1)}, bf16[8,56,256]{2,1,0:T(8,128)(2,1)S(1)}, u32[]{:S(2)}, u32[]{:S(2)}) collective-permute-start(bf16[8,56,256]{2,1,0:T(8,128)(2,1)S(1)} %collective-permute-done.2), channel_id=1, source_target_pairs={{0,28},{4,0},{8,4},{12,8},{16,12},{20,16},{24,20},{28,24},{1,29},{... | collective-permute-start | bytes 688136 | tf_op jit(solution)/shard_map/ppermute | solution.py:284
  31.2 6.4 %collective-permute-start.1 = (bf16[8,56,256]{2,1,0:T(8,128)(2,1)S(1)}, bf16[8,56,256]{2,1,0:T(8,128)(2,1)S(1)}, u32[]{:S(2)}, u32[]{:S(2)}) collective-permute-start(bf16[8,56,256]{2,1,0:T(8,128)(2,1)S(1)} %collective-permute-done), channel_id=1, source_target_pairs={{0,4},{4,8},{8,12},{12,16},{16,20},{20,24},{24,28},{28,0},{1,5},{5... | collective-permute-start | bytes 688136 | tf_op jit(solution)/shard_map/ppermute | solution.py:284
  37.6 10.1 %collective-permute-start.5 = (bf16[8,56,256]{2,1,0:T(8,128)(2,1)S(1)}, bf16[8,56,256]{2,1,0:T(8,128)(2,1)S(1)}, u32[]{:S(2)}, u32[]{:S(2)}) collective-permute-start(bf16[8,56,256]{2,1,0:T(8,128)(2,1)S(1)} %collective-permute-done.1), channel_id=1, source_target_pairs={{0,4},{4,8},{8,12},{12,16},{16,20},{20,24},{24,28},{28,0},{1,5},{5... | collective-permute-start | bytes 688136 | tf_op jit(solution)/shard_map/ppermute | solution.py:284
  37.7 10.0 %collective-permute-start.6 = (bf16[8,56,256]{2,1,0:T(8,128)(2,1)S(1)}, bf16[8,56,256]{2,1,0:T(8,128)(2,1)S(1)}, u32[]{:S(2)}, u32[]{:S(2)}) collective-permute-start(bf16[8,56,256]{2,1,0:T(8,128)(2,1)S(1)} %collective-permute-done.3), channel_id=1, source_target_pairs={{0,28},{4,0},{8,4},{12,8},{16,12},{20,16},{24,20},{28,24},{1,29},{... | collective-permute-start | bytes 688136 | tf_op jit(solution)/shard_map/ppermute | solution.py:284
  40.5 7.5 %collective-permute-start.8 = (bf16[4,56,256]{2,1,0:T(8,128)(2,1)S(1)}, bf16[4,56,256]{2,1,0:T(8,128)(2,1)S(1)}, u32[]{:S(2)}, u32[]{:S(2)}) collective-permute-start(bf16[4,56,256]{2,1,0:T(8,128)(2,1)S(1)} %slice.15), channel_id=1, source_target_pairs={{0,24},{4,28},{8,0},{12,4},{16,8},{20,12},{24,16},{28,20},{1,25},{... | collective-permute-start | bytes 344072 | tf_op jit(solution)/shard_map/ppermute | solution.py:284
  40.5 7.5 %collective-permute-start.7 = (bf16[4,56,256]{2,1,0:T(8,128)(2,1)S(1)}, bf16[4,56,256]{2,1,0:T(8,128)(2,1)S(1)}, u32[]{:S(2)}, u32[]{:S(2)}) collective-permute-start(bf16[4,56,256]{2,1,0:T(8,128)(2,1)S(1)} %slice.14), channel_id=1, source_target_pairs={{0,8},{4,12},{8,16},{12,20},{16,24},{20,28},{24,0},{28,4},{1,9},{5... | collective-permute-start | bytes 344072 | tf_op jit(solution)/shard_map/ppermute | solution.py:284
  42.9 11.2 %collective-permute-start.9 = (bf16[40,56,256]{2,1,0:T(8,128)(2,1)S(1)}, bf16[40,56,256]{2,1,0:T(8,128)(2,1)S(1)}, u32[]{:S(2)}, u32[]{:S(2)}) collective-permute-start(bf16[40,56,256]{2,1,0:T(8,128)(2,1)S(1)} %constant_dynamic-update-slice_fusion.refs_4_), channel_id=1, source_target_pairs={{0,64},{64,0},{1,65},{65,1},{2,66},{66,2},{3,67},{67,3},{4,68},{68... | collective-permute-start | bytes 3440648 | tf_op jit(solution)/shard_map/ppermute | solution.py:284
  48.0 6.0 %collective-permute-start.10 = (bf16[24,56,256]{2,1,0:T(8,128)(2,1)S(1)}, bf16[24,56,256]{2,1,0:T(8,128)(2,1)S(1)}, u32[]{:S(2)}, u32[]{:S(2)}) collective-permute-start(bf16[24,56,256]{2,1,0:T(8,128)(2,1)S(1)} %constant_dynamic-update-slice_fusion.5.refs_5_), channel_id=1, source_target_pairs={{0,64},{64,0},{1,65},{65,1},{2,66},{66,2},{3,67},{67,3},{4,68},{68... | collective-permute-start | bytes 2064392 | tf_op jit(solution)/shard_map/ppermute | solution.py:284
